TPU v7x, 32 devices: a whole 2x2x4 slice. The times are simulated.
32 devices in a mesh: dp: 8 (over z, core), seq: 4 (over y, x).
Axes of the slice: x: 2, y: 2, z: 4, core: 2. Of those that a mesh axis runs over, the one named last changes fastest.
Arguments:
- inputs: bfloat16 [8, 2048, 1024], P('dp', 'seq'), may hold values from -6 to 6
- segments: int32 [8, 2048], P('dp'), may hold values from 0 to 34, as said below
- cotangent: bfloat16 [8, 2048, 1024], P('dp', 'seq'), may hold values from -6 to 6
- norm_gain_mix: float32 [1024], replicated, may hold values from 0.5 to 1.5
- w_query: float32 [1024, 1024], P('dp'), may hold values from -0.1875 to 0.1875
- w_key: float32 [1024, 1024], P('dp'), may hold values from -0.1875 to 0.1875
- w_value: float32 [1024, 2048], P('dp'), may hold values from -0.1875 to 0.1875
- w_outgate: float32 [1024, 2048], P('dp'), may hold values from -0.1875 to 0.1875
- w_gates: float32 [1024, 16], P('dp'), may hold values from -0.1875 to 0.1875
- conv_weight: float32 [4, 4096], replicated, may hold values from -3 to 3
- decay_log: float32 [8], replicated, may hold values from 0 to 2.77
- dt_bias: float32 [8], replicated, may hold values from -6.9 to -2.25
- out_norm_gain: float32 [256], replicated, may hold values from 0.5 to 1.5
- w_out: float32 [2048, 1024], P(None, 'dp'), may hold values from -0.25 to 0.25
- norm_gain_ffn: float32 [1024], replicated, may hold values from 0.5 to 1.5
- w_ffn_gate: float32 [1024, 2816], P('dp'), may hold values from -0.1875 to 0.1875
- w_ffn_up: float32 [1024, 2816], P('dp'), may hold values from -0.1875 to 0.1875
- w_ffn_down: float32 [2816, 1024], P(None, 'dp'), may hold values from -0.21875 to 0.21875
Outputs:
- output: bfloat16 [8, 2048, 1024], P('dp', 'seq')
- grad_inputs: float32 [8, 2048, 1024], P('dp', 'seq')
- grad_norm_gain_mix: float32 [1024], replicated
- grad_w_query: float32 [1024, 1024], P('dp')
- grad_w_key: float32 [1024, 1024], P('dp')
- grad_w_value: float32 [1024, 2048], P('dp')
- grad_w_outgate: float32 [1024, 2048], P('dp')
- grad_w_gates: float32 [1024, 16], P('dp')
- grad_conv_weight: float32 [4, 4096], replicated
- grad_decay_log: float32 [8], replicated
- grad_dt_bias: float32 [8], replicated
- grad_out_norm_gain: float32 [256], replicated
- grad_w_out: float32 [2048, 1024], P(None, 'dp')
- grad_norm_gain_ffn: float32 [1024], replicated
- grad_w_ffn_gate: float32 [1024, 2816], P('dp')
- grad_w_ffn_up: float32 [1024, 2816], P('dp')
- grad_w_ffn_down: float32 [2816, 1024], P(None, 'dp')
Inputs may be any that keep to these rules, and one draw needn't show every extreme that they name: `segments`: per row, segment numbers start at 0, never fall, and rise by one at each document's first token; each row holds exactly 35 documents; one document of each row begins within the first 512 tokens and ends within the last 512.
All inputs are finite; a program needn't handle non-finite values.
Results may differ from a plain program's by a relative error of at most 0.019.
Values may be sent and summed in bfloat16 or wider, within the bound.
A program may use at most 448 MiB of HBM per device.

v0:
```python
import functools

import jax
import jax.numpy as jnp
from jax import lax
from jax.experimental import pallas as pl
from jax.experimental.pallas import tpu as pltpu
from jax.sharding import PartitionSpec as P

H = 8
DK = 128
DV = 256
CONV = 4
HALO = 16
CHUNK = 128
HC = 2 * DK + DV
LANES = 128
PLANES, CORES, SPOTS = 4, 2, 4

AT_LOGIT = H * HC
AT_GATE = AT_LOGIT + 512
AT_OUT = AT_GATE + H * DV
AT_FFN = AT_OUT + H * DV
VMEM_LIMIT = 62 * 2**20

F32 = jnp.float32
BF16 = jnp.bfloat16
NN = ((1,), (0,))
NT = ((1,), (1,))
TN = ((0,), (0,))


def mm(left, right, dims=NN):
    return lax.dot_general(
        left.astype(BF16), right.astype(BF16), (dims, ((), ())), preferred_element_type=F32
    )


def mm_exact(left, right, dims=NN):
    return lax.dot_general(
        left, right, (dims, ((), ())), precision=lax.Precision.HIGHEST, preferred_element_type=F32
    )


def halves(value):
    high = value.astype(BF16)
    return high, (value - high.astype(F32)).astype(BF16)


def mm_three(left, right):
    left_high, left_low = halves(left)
    right_high, right_low = halves(right)
    return mm(left_high, right_high) + (mm(left_high, right_low) + mm(left_low, right_high))


def params(**more):
    return pltpu.CompilerParams(vmem_limit_bytes=VMEM_LIMIT, **more)


def cost(flops, nbytes):
    return pl.CostEstimate(flops=int(flops), bytes_accessed=int(nbytes), transcendentals=0)


def iota2(shape, axis):
    return lax.broadcasted_iota(jnp.int32, shape, axis)


def lane(value, index):
    picked = jnp.where(iota2(value.shape, 1) == index, value, 0.0)
    return jnp.sum(picked, axis=1, keepdims=True)


def to_row(column):
    size = column.shape[0]
    same = iota2((size, size), 0) == iota2((size, size), 1)
    return jnp.sum(jnp.where(same, column, 0.0), axis=0, keepdims=True)


def to_column(row):
    size = row.shape[1]
    same = iota2((size, size), 0) == iota2((size, size), 1)
    return jnp.sum(jnp.where(same, row, 0.0), axis=1, keepdims=True)


def outgate_kernel(h_ref, w_ref, g_ref):
    g_ref[...] = mm(h_ref[HALO:, :], w_ref[...])


def outgate(hidden, weights):
    rows, width = hidden.shape
    cols = H * DV
    block = 512
    return pl.pallas_call(
        outgate_kernel,
        grid=(cols // block,),
        in_specs=[
            pl.BlockSpec((rows, width), lambda j: (0, 0)),
            pl.BlockSpec((width, block), lambda j: (0, j + AT_GATE // block)),
        ],
        out_specs=pl.BlockSpec((rows - HALO, block), lambda j: (0, j)),
        out_shape=jax.ShapeDtypeStruct((rows - HALO, cols), F32),
        compiler_params=params(),
        cost_estimate=cost(2 * rows * width * cols, 2 * width * cols + 4 * rows * cols),
        name="outgate",
    )(hidden, weights)


def outer_kernel(left_ref, right_ref, out_ref, turn_ref, *, skip):
    @pl.when(pl.program_id(0) == 0)
    def _():
        turn_ref[...] = jnp.transpose(left_ref[skip:, :])

    out_ref[...] = mm(turn_ref[...], right_ref[...]).astype(BF16)


def outer(left, right, skip):
    rows, width = left.shape
    cols = right.shape[1]
    block = next(b for b in (512, 256, 128) if cols % b == 0)
    return pl.pallas_call(
        functools.partial(outer_kernel, skip=skip),
        grid=(cols // block,),
        in_specs=[
            pl.BlockSpec((rows, width), lambda j: (0, 0)),
            pl.BlockSpec((rows - skip, block), lambda j: (0, j)),
        ],
        out_specs=pl.BlockSpec((width, block), lambda j: (0, j)),
        out_shape=jax.ShapeDtypeStruct((width, cols), BF16),
        scratch_shapes=[pltpu.VMEM((width, rows - skip), BF16)],
        compiler_params=params(),
        cost_estimate=cost(2 * rows * width * cols, 2 * width * cols + 2 * rows * cols),
        name="outer",
    )(left, right)


def gate_tables(logit_ref, par_ref, beta_ref, decay_ref, cum_ref):
    logits = logit_ref[HALO:, :]
    beta_ref[...] = jax.nn.sigmoid(logits)
    shifted = logits + par_ref[1:2, :]
    soft = jnp.maximum(shifted, 0.0) + jnp.log1p(jnp.exp(-jnp.abs(shifted)))
    decay_ref[...] = -jnp.exp(par_ref[0:1, :]) * soft
    lower = (iota2((CHUNK, CHUNK), 0) >= iota2((CHUNK, CHUNK), 1)).astype(F32)
    for c in range(logits.shape[0] // CHUNK):
        part = decay_ref[c * CHUNK : (c + 1) * CHUNK, :]
        cum_ref[c * CHUNK : (c + 1) * CHUNK, :] = mm_exact(lower, part)


def mix_taps(p_ref, taps_ref, cols, pf_ref):
    tokens = cols.shape[0]
    pf_ref[...] = p_ref[...].astype(F32)
    total = pf_ref[HALO:, :] * taps_ref[0:1, :]
    for j in range(1, CONV):
        total += pf_ref[HALO - j : HALO - j + tokens, :] * taps_ref[j : j + 1, :] * cols[:, j : j + 1]
    return total


def chunk_tables(c, head, cols, segr_ref, cum_ref):
    rows = slice(c * CHUNK, (c + 1) * CHUNK)
    cum = lane(cum_ref[rows, :], head)
    cum_row = to_row(cum)
    same = cols[rows, 0:1] == segr_ref[0:1, rows]
    row_ids, col_ids = iota2((CHUNK, CHUNK), 0), iota2((CHUNK, CHUNK), 1)
    gamma = jnp.where((row_ids >= col_ids) & same, jnp.exp(jnp.minimum(cum - cum_row, 0.0)), 0.0)
    strict = jnp.where(row_ids > col_ids, gamma, 0.0)
    carry = jnp.exp(cum) * cols[rows, 4:5]
    last = jnp.exp(cum[CHUNK - 1 :, :] - cum) * cols[rows, 5:6]
    return gamma, strict, carry, last


def unit_lower_inverses(systems):
    size = systems[0].shape[0]
    row_ids, col_ids = iota2((size, size), 0), iota2((size, size), 1)
    eye = (row_ids == col_ids).astype(F32)
    found = [eye - jnp.where(row_ids // 2 == col_ids // 2, low, 0.0) for low in systems]
    width = 2
    while width < size:
        joined = (row_ids // (2 * width) == col_ids // (2 * width)) & (
            row_ids // width != col_ids // width
        )
        first = [mm_three(jnp.where(joined, low, 0.0), inv) for low, inv in zip(systems, found)]
        found = [inv - mm_three(inv, part) for inv, part in zip(found, first)]
        width *= 2
    return found


def flip_spot(value, bits):
    low, high = lax.rem(value, 2), value // 2
    flip = lambda one, other: one + other - 2 * one * other
    return flip(low, bits % 2) + 2 * flip(high, bits // 2)


def device(planes=0, core=0, spot=0):
    place, here = lax.axis_index("dp"), lax.axis_index("seq")
    z = lax.rem(place // CORES + planes, PLANES)
    return {"dp": z * CORES + flip_spot(lax.rem(place, CORES), core), "seq": flip_spot(here, spot)}


def greet(partners):
    barrier = pltpu.get_barrier_semaphore()
    for partner in partners:
        pl.semaphore_signal(barrier, inc=1, device_id=device(**partner), device_id_type=pl.DeviceIdType.MESH)
    pl.semaphore_wait(barrier, len(partners))


def gather_spans(inner):
    spans = [((H - 1) * HC, HC + LANES), ((H - 2) * HC, HC)]
    spans += [(h * HC, 2 * HC) for h in (4, 2, 0)]
    for at, size in ((AT_GATE, H * DV), (AT_OUT, H * DV)) + tuple((AT_FFN + i * inner, inner) for i in range(3)):
        spans += [(at + low, min(1024, size - low)) for low in range(0, size, 1024)]
    return spans


class Gathering:
    STAGES = (0, 1, 2, 3, 5, 7, 8)
    FIRST = ((0, 1, 2, 3, 4, 5, 6), (0, 1, 2, 3, 4, 6, 7))

    def __init__(self, spans, shard_ref, full_ref, sems, pack):
        self.spans, self.shard, self.full, self.pack = spans, shard_ref, full_ref, pack
        self.send_sem, self.recv_sem, self.local_sem = sems
        self.piece = shard_ref.shape[0] // SPOTS
        self.half = full_ref.shape[0] // CORES
        self.z = lax.axis_index("dp") // CORES

    def quarter(self, spot, cols):
        row = flip_spot(lax.axis_index("seq"), spot) * self.piece
        return self.shard.at[pl.ds(pl.multiple_of(row, self.piece), self.piece), cols]

    def own(self, group):
        at, size = self.spans[group]
        cols = pl.ds(at, size)
        block = PLANES * self.piece
        return [
            pltpu.make_async_copy(
                self.quarter(q, cols),
                self.full.at[q * block : q * block + self.piece, cols],
                self.local_sem.at[group, q],
            )
            for q in range(SPOTS)
        ]

    def copy(self, group, kind):
        at, size = self.spans[group]
        cols = pl.ds(at, size)
        piece, full = self.piece, self.full
        block = PLANES * piece
        rows = lambda quarter: pl.ds(quarter * block + piece, block - piece)
        if kind < 6:
            read, step, written = ((0, 1, 1), (0, -1, 3), (1, 1, 2), (3, -1, 2), (2, 1, 3), (2, -1, 1))[kind]
            source = self.quarter(0, cols) if read == 0 else full.at[read * piece : (read + 1) * piece, cols]
            target = full.at[written * piece : (written + 1) * piece, cols]
            to, arrival = device(planes=step % PLANES), written - 1
        elif kind < 8:
            source = full.at[rows(0), cols]
            target = full.at[rows(kind - 5), cols]
            to, arrival = device(spot=kind - 5), kind - 3
        elif kind == 8:
            by = 1 + group % 2
            source = full.at[rows(by), cols]
            target = full.at[rows(3), cols]
            to, arrival = device(spot=3 - by), 5
        else:
            source = full.at[0 : self.half, cols]
            target = full.at[self.half : 2 * self.half, cols]
            to, arrival = device(core=1), 6
        return pltpu.make_async_remote_copy(
            src_ref=source,
            dst_ref=target,
            send_sem=self.send_sem.at[group, kind],
            recv_sem=self.recv_sem.at[group, arrival],
            device_id=to,
            device_id_type=pl.DeviceIdType.MESH,
        )

    def sends(self, kind):
        z = self.z
        return (z < 3, z > 0, (z > 0) & (z < 3), (z > 0) & (z < 3), z == 2, z == 1)[kind]

    def start(self, group, kind):
        @pl.when(self.sends(kind))
        def _():
            self.copy(group, kind).start()

    def arrive(self, group, kind, condition):
        @pl.when(condition)
        def _():
            self.copy(group, kind).wait_recv()

    def tick(self, at):
        z = self.z
        due = []
        for group in range(len(self.spans)):
            stages = (self.FIRST + (self.STAGES,) * len(self.spans))[group]
            due += [(stage, group) for stage in range(len(stages)) if group + stages[stage] == at]
        for stage, group in sorted(due, reverse=True):
            by = 1 + group % 2
            if stage == 0:
                self.pack(*self.spans[group])
                self.start(group, 0)
                self.start(group, 1)
                for local in self.own(group):
                    local.start()
            elif stage == 1:
                self.arrive(group, 0, z > 0)
                self.start(group, 2)
                self.arrive(group, 1, z < 3)
                self.start(group, 3)
            elif stage == 2:
                self.copy(group, 2).wait_recv()
                self.start(group, 4)
                self.start(group, 5)
            elif stage == 3:
                self.arrive(group, 0, z == 0)
                self.arrive(group, 1, z == 3)
                self.copy(group, 5 + by).start()
                self.copy(group, 8 - by).start()
            elif stage == 4:
                self.copy(group, 5 + by).wait_recv()
                self.copy(group, 8).start()
            elif stage == 5:
                self.copy(group, 8 - by).wait_recv()
                self.copy(group, 8).wait_recv()
                for local in self.own(group):
                    local.wait()
                self.copy(group, 9).start()
            else:
                self.copy(group, 9).wait_recv()

    def finish(self):
        for group in range(len(self.spans)):
            for kind in range(6):

                @pl.when(self.sends(kind))
                def _(group=group, kind=kind):
                    self.copy(group, kind).wait_send()

            for kind in range(6, 10):
                self.copy(group, kind).wait_send()


def forward_kernel(
    h_ref, full_ref, taps_ref, par_ref, cols_ref, segr_ref,
    p_ref, logit_ref, part_ref, resp_ref, exch_ref, inv_ref, upd_ref, st_ref, stm_ref, amap_ref, rmap_ref,
    beta_ref, decay_ref, cum_ref, pf_ref, mix_ref, w_ref, wl_ref, load_sem,
):
    head = pl.program_id(0)
    load_head(head, h_ref, full_ref, par_ref, p_ref, logit_ref, beta_ref, decay_ref, cum_ref, w_ref, wl_ref, load_sem)
    state = forward_head(
        head, p_ref, taps_ref, cols_ref, segr_ref, part_ref, resp_ref, inv_ref, upd_ref, st_ref, stm_ref,
        amap_ref, rmap_ref, beta_ref, cum_ref, pf_ref, mix_ref, lambda: None,
    )
    exch_ref[0, 0] = state.astype(BF16)


def load_head(
    head, h_ref, full_ref, par_ref, p_ref, logit_ref, beta_ref, decay_ref, cum_ref, w_ref, wl_ref, load_sem
):
    def load(slot, at, size, to):
        return pltpu.make_async_copy(full_ref.at[:, pl.ds(at, size)], to, load_sem.at[slot])

    mine = load(0, pl.multiple_of((H - 1 - head) * HC, HC), HC, w_ref)
    mine.start()

    @pl.when(head == 0)
    def _():
        gates = load(1, AT_LOGIT, LANES, wl_ref)
        gates.start()
        gates.wait()
        logit_ref[...] = mm(h_ref[...], wl_ref[...])
        gate_tables(logit_ref, par_ref, beta_ref, decay_ref, cum_ref)

    mine.wait()
    p_ref[...] = mm(h_ref[...], w_ref[...]).astype(BF16)


def forward_head(
    head, p_ref, taps_ref, cols_ref, segr_ref, part_ref, resp_ref, inv_ref, upd_ref, st_ref, stm_ref,
    amap_ref, rmap_ref, beta_ref, cum_ref, pf_ref, mix_ref, between,
):
    cols = cols_ref[...]
    tokens = cols.shape[0]
    total = mix_taps(p_ref, taps_ref, cols, pf_ref)
    mix_ref[...] = total * jax.nn.sigmoid(total)
    between()
    beta = lane(beta_ref[...], head + H)
    chunks = range(tokens // CHUNK)
    tables, lows, keys, queries = [], [], [], []
    for c in chunks:
        rows = slice(c * CHUNK, (c + 1) * CHUNK)
        query = mix_ref[rows, :DK]
        query = query * (lax.rsqrt(jnp.sum(query * query, axis=1, keepdims=True) + 1e-06) * DK**-0.5)
        key = mix_ref[rows, DK : 2 * DK]
        key = key * lax.rsqrt(jnp.sum(key * key, axis=1, keepdims=True) + 1e-06)
        gamma, strict, carry, last = chunk_tables(c, head, cols, segr_ref, cum_ref)
        dots = mm(jnp.concatenate([key, query], axis=0), key, NT)
        lows.append(beta[rows] * strict * dots[:CHUNK])
        tables.append((gamma * dots[CHUNK:], carry, last))
        keys.append(key)
        queries.append(query)
    inverses = unit_lower_inverses(lows)
    state = None
    for c in chunks:
        rows = slice(c * CHUNK, (c + 1) * CHUNK)
        scores, carry, last = tables[c]
        key, query = keys[c], queries[c]
        target = jnp.concatenate([mix_ref[rows, 2 * DK :], carry * key], axis=1) * beta[rows]
        updates = mm(inverses[c], target)
        inv_ref[0, c] = inverses[c].astype(BF16)
        upd_ref[0, rows, :] = updates
        weighted_t = jnp.transpose(last * key)
        both = mm(jnp.concatenate([weighted_t, scores], axis=0), updates)
        eye = (iota2((DK, DK), 0) == iota2((DK, DK), 1)).astype(F32)
        step_map = carry[CHUNK - 1 :, :] * eye - both[:DK, DV:]
        read_map = carry * query - both[DK:, DV:]
        amap_ref[0, c] = step_map.astype(BF16)
        rmap_ref[0, c] = read_map.astype(BF16)
        if c == 0:
            st_ref[0, c] = jnp.zeros((DK, DV), F32)
            stm_ref[0, c] = eye.astype(BF16)
            part_ref[rows, :] = both[DK:, :DV]
            resp_ref[rows, :] = read_map.astype(BF16)
            state = jnp.concatenate([both[:DK, :DV], step_map], axis=1)
        else:
            st_ref[0, c] = state[:, :DV]
            stm_ref[0, c] = state[:, DV:].astype(BF16)
            moved = mm(jnp.concatenate([step_map, read_map], axis=0), state)
            part_ref[rows, :] = both[DK:, :DV] + moved[DK:, :DV]
            resp_ref[rows, :] = moved[DK:, DV:].astype(BF16)
            state = moved[:DK] + jnp.concatenate(
                [both[:DK, :DV], jnp.zeros((DK, DK), F32)], axis=1
            )
    return state


def delta_forward(hidden, weights, taps, par, cols, segr):
    rows, width = hidden.shape
    tokens = rows - HALO
    chunks = tokens // CHUNK
    whole = lambda shape: pl.BlockSpec(shape, lambda h: (0,) * len(shape))
    by_head = lambda shape: pl.BlockSpec(shape, lambda h: (h,) + (0,) * (len(shape) - 1))
    return pl.pallas_call(
        forward_kernel,
        grid=(H,),
        in_specs=[
            whole((rows, width)),
            pl.BlockSpec(memory_space=pl.ANY),
            pl.BlockSpec((8, HC), lambda h: (0, h)),
            whole((8, LANES)),
            whole((tokens, LANES)),
            whole(segr.shape),
        ],
        out_specs=[
            pl.BlockSpec((rows, HC), lambda h: (0, h)),
            whole((rows, LANES)),
            pl.BlockSpec((tokens, DV), lambda h: (0, h)),
            pl.BlockSpec((tokens, DK), lambda h: (0, h)),
            pl.BlockSpec((1, 1, DK, DV + DK), lambda h: (0, h, 0, 0)),
            by_head((1, chunks, CHUNK, CHUNK)),
            by_head((1, tokens, DV + DK)),
            by_head((1, chunks, DK, DV)),
            by_head((1, chunks, DK, DK)),
            by_head((1, chunks, DK, DK)),
            by_head((1, chunks, CHUNK, DK)),
        ],
        out_shape=[
            jax.ShapeDtypeStruct((rows, H * HC), BF16),
            jax.ShapeDtypeStruct((rows, LANES), F32),
            jax.ShapeDtypeStruct((tokens, H * DV), F32),
            jax.ShapeDtypeStruct((tokens, H * DK), BF16),
            jax.ShapeDtypeStruct((1, H, DK, DV + DK), BF16),
        ]
        + saved_shapes(chunks),
        scratch_shapes=[
            pltpu.VMEM((tokens, LANES), F32),
            pltpu.VMEM((tokens, LANES), F32),
            pltpu.VMEM((tokens, LANES), F32),
            pltpu.VMEM((rows, HC), F32),
            pltpu.VMEM((tokens, HC), F32),
            pltpu.VMEM((width, HC), BF16),
            pltpu.VMEM((width, LANES), BF16),
            pltpu.SemaphoreType.DMA((2,)),
        ],
        compiler_params=params(),
        cost_estimate=cost(6e9 * H, 5e6 * H),
        name="delta_forward",
    )(hidden, weights, taps, par, cols, segr)


def saved_shapes(chunks):
    return [
        jax.ShapeDtypeStruct((H, chunks, CHUNK, CHUNK), BF16),
        jax.ShapeDtypeStruct((H, chunks * CHUNK, DV + DK), F32),
        jax.ShapeDtypeStruct((H, chunks, DK, DV), F32),
        jax.ShapeDtypeStruct((H, chunks, DK, DK), BF16),
        jax.ShapeDtypeStruct((H, chunks, DK, DK), BF16),
        jax.ShapeDtypeStruct((H, chunks, CHUNK, DK), BF16),
    ]


def mixer_forward_kernel(
    x_ref, cot_ref, wq_ref, wk_ref, wv_ref, wo_ref, wl_in, wm_ref, wg_ref, wu_ref, wd_ref,
    gains_ref, gain_ref, taps_ref, par_ref, near_ref, later_ref,
    full_ref, hidden_out, x_out, cot_out, turn_out, y_out, mid_out,
    gains_out, cols_ref, back_ref, p_ref, logit_ref, resp_out,
    inv_ref, upd_ref, st_ref, stm_ref, amap_ref, rmap_ref, maps_ref, sin_ref, attn_ref, gpre_ref, gated_ref,
    shard_ref, hidden_ref, xs_ref, cots_ref, turn_ref, y_ref, mid_ref, xh_ref, part_ref, resp_ref, exch_ref, stage_ref, half_ref, low_ref,
    beta_ref, decay_ref, cum_ref, pf_ref, mix_ref, w_ref, wl_ref, wb_ref,
    send_sem, recv_sem, local_sem, exch_send, exch_recv, load_sem, pair_sem, out_sem, halo_sem, *, spans, inner,
):
    step = pl.program_id(0)
    place = lax.axis_index("seq")
    tokens, width = x_ref.shape

    def pack(at, size):
        while size > 0:
            if at < AT_LOGIT:
                head, span = H - 1 - at // HC, HC
                shard_ref[:, at : at + DK] = wq_ref[:, head * DK : (head + 1) * DK].astype(BF16)
                shard_ref[:, at + DK : at + 2 * DK] = wk_ref[:, head * DK : (head + 1) * DK].astype(BF16)
                shard_ref[:, at + 2 * DK : at + HC] = wv_ref[:, head * DV : (head + 1) * DV].astype(BF16)
            elif at < AT_GATE:
                span = LANES
                shard_ref[:, at : at + LANES] = jnp.zeros((shard_ref.shape[0], LANES), BF16)
                shard_ref[:, at : at + 2 * H] = wl_in[...].astype(BF16)
            elif at < AT_OUT:
                span, low = size, at - AT_GATE
                shard_ref[:, at : at + span] = wo_ref[:, low : low + span].astype(BF16)
            elif at < AT_FFN:
                span, low = size, at - AT_OUT
                shard_ref[:, at : at + span] = jnp.transpose(wm_ref[low : low + span, :]).astype(BF16)
            else:
                span, which, low = size, (at - AT_FFN) // inner, (at - AT_FFN) % inner
                if which < 2:
                    shard_ref[:, at : at + span] = (wg_ref, wu_ref)[which][:, low : low + span].astype(BF16)
                else:
                    shard_ref[:, at : at + span] = jnp.transpose(wd_ref[low : low + span, :]).astype(BF16)
            at, size = at + span, size - span

    gathering = Gathering(spans, shard_ref, full_ref, (send_sem, recv_sem, local_sem), pack)
    lead = gathering.FIRST[0][-1] + 1
    final_tick = len(spans) + gathering.STAGES[-1]

    upper = place // 2 == 1
    second = lax.rem(place, 2) == 1

    def give(h):
        return pltpu.make_async_remote_copy(
            src_ref=stage_ref.at[h],
            dst_ref=exch_ref.at[h],
            send_sem=exch_send.at[0, h],
            recv_sem=exch_recv.at[0, h],
            device_id=device(spot=1),
            device_id_type=pl.DeviceIdType.MESH,
        )

    def give_half(h):
        return pltpu.make_async_remote_copy(
            src_ref=half_ref.at[h],
            dst_ref=low_ref.at[h],
            send_sem=exch_send.at[1, h],
            recv_sem=exch_recv.at[1, h],
            device_id=device(spot=2),
            device_id_type=pl.DeviceIdType.MESH,
        )

    def join(h):
        give(h).wait()

        @pl.when(jnp.logical_not(upper))
        def _():
            mine, theirs = stage_ref[h], exch_ref[h]
            later = jnp.where(second, mine, theirs)
            earlier = jnp.where(second, theirs, mine)
            half_ref[h] = (later[:, :DV].astype(F32) + mm(later[:, DV:], earlier[:, :DV])).astype(BF16)
            give_half(h).start()

    def give_halo():
        return pltpu.make_async_remote_copy(
            src_ref=x_ref.at[tokens - HALO : tokens],
            dst_ref=xh_ref,
            send_sem=halo_sem.at[0],
            recv_sem=halo_sem.at[1],
            device_id={"dp": lax.axis_index("dp"), "seq": lax.rem(place + 1, SPOTS)},
            device_id_type=pl.DeviceIdType.MESH,
        )

    def keep(which):
        source, to = (
            (hidden_ref, hidden_out), (xs_ref, x_out), (cots_ref, cot_out), (turn_ref, turn_out),
            (y_ref, y_out), (mid_ref, mid_out),
        )[which]
        return pltpu.make_async_copy(source, to, out_sem.at[which])

    def load_pair(h):
        slot = lax.rem(h, 2)
        return [
            pltpu.make_async_copy(
                full_ref.at[:, pl.ds(pl.multiple_of(at + h * DV, DV), DV)], wb_ref.at[slot, i], pair_sem.at[slot, i]
            )
            for i, at in enumerate((AT_GATE, AT_OUT))
        ]

    @pl.when(step == 0)
    def _():
        greet([dict(planes=d) for d in (1, 2, 3)] + [dict(spot=s) for s in (1, 2, 3)] + [dict(core=1)])

        @pl.when(place < SPOTS - 1)
        def _():
            give_halo().start()

        gathering.tick(0)
        at = iota2((1, width), 1)
        piece = width // (PLANES * CORES * SPOTS)
        core, rest = at // (width // 2), at % (width // 2)
        quarter, plane, low = rest // (PLANES * piece), rest // piece % PLANES, rest % piece
        place_dp = lax.axis_index("dp")
        z, c = place_dp // CORES, lax.rem(place_dp, CORES)
        chip = ((z - plane + PLANES) % PLANES) * CORES + (c + core - 2 * c * core)
        order = (chip * SPOTS + flip_spot(quarter, place)) * piece + low
        turn_ref[...] = jnp.where(iota2((width, width), 0) == order, 1.0, 0.0).astype(BF16)
        keep(3).start()
        gathering.tick(1)
        cots_ref[...] = mm(cot_ref[...], turn_ref[...]).astype(BF16)
        keep(2).start()
        high, mid = halves(gains_ref[...])
        rest = (gains_ref[...] - high.astype(F32)) - mid.astype(F32)
        gains_out[...] = mm(high, turn_ref[...]) + mm(mid, turn_ref[...]) + mm(rest, turn_ref[...])
        gathering.tick(2)
        blank = jnp.zeros((LANES - near_ref.shape[0], LANES), F32)
        for n in range(tokens // LANES):
            span = slice(n * LANES, (n + 1) * LANES)
            cols_ref[span, :] = jnp.transpose(jnp.concatenate([near_ref[:, span], blank], axis=0))
        for n in range(tokens // LANES + 1):
            span = slice(n * LANES, (n + 1) * LANES)
            turned = jnp.transpose(jnp.concatenate([later_ref[:, span], blank], axis=0))
            kept = min(LANES, tokens + HALO - n * LANES)
            back_ref[n * LANES : n * LANES + kept, :] = turned[:kept]
        gathering.tick(3)

        @pl.when(place > 0)
        def _():
            give_halo().wait_recv()

        @pl.when(place == 0)
        def _():
            xh_ref[...] = jnp.zeros_like(xh_ref)

        value = mm(jnp.concatenate([xh_ref[...], x_ref[...]], axis=0), turn_ref[...])
        xs_ref[...] = value[HALO:].astype(BF16)
        keep(1).start()
        size = lax.rsqrt(jnp.mean(value * value, axis=-1, keepdims=True) + 1e-06)
        hidden_ref[...] = (value * size * gains_out[0:1, :]).astype(BF16)
        keep(0).start()
        for at in range(4, lead):
            gathering.tick(at)

    @pl.when((step >= 2) & (step < H + 2))
    def _():
        join(step - 2)

    @pl.when(step < H)
    def _():
        head = step
        for h in range(1, H):

            @pl.when(head == h)
            def _(h=h):
                gathering.tick(lead + 2 * h - 1)

        load_head(
            head, hidden_ref, full_ref, par_ref, p_ref, logit_ref, beta_ref, decay_ref, cum_ref, w_ref, wl_ref, load_sem
        )

        def between():
            for h in range(H):

                @pl.when(head == h)
                def _(h=h):
                    gathering.tick(lead + 2 * h)

        state = forward_head(
            head, p_ref, taps_ref, cols_ref, near_ref, part_ref.at[head], resp_ref.at[head], inv_ref, upd_ref,
            st_ref, stm_ref, amap_ref, rmap_ref, beta_ref, cum_ref, pf_ref, mix_ref, between,
        )
        resp_out[...] = resp_ref[head]
        stage_ref[head] = state.astype(BF16)
        give(head).start()

        @pl.when(head == H - 1)
        def _():
            for copy in load_pair(0):
                copy.start()

    @pl.when(step >= H)
    def _():
        head = step - H
        for n, at in enumerate(range(lead + 2 * H - 1, final_tick)):

            @pl.when(head == min(n, H - 1))
            def _(at=at):
                gathering.tick(at)

        @pl.when(head < H - 1)
        def _():
            for copy in load_pair(head + 1):
                copy.start()

        for copy in load_pair(head):
            copy.wait()
        @pl.when(upper)
        def _():
            give_half(head).wait_recv()

        @pl.when(jnp.logical_not(upper))
        def _():
            low_ref[head] = jnp.zeros((DK, DV), BF16)
            give_half(head).wait_send()

        slot = lax.rem(head, 2)
        gate = mm(hidden_ref[HALO:, :], wb_ref[slot, 0])
        gpre_ref[...] = gate
        theirs = exch_ref[head]
        maps_ref[0, 0] = stage_ref[head, :, DV:]
        maps_ref[1, 0] = theirs[:, DV:]
        state = low_ref[head].astype(F32)
        state = jnp.where(second, theirs[:, :DV].astype(F32) + mm(theirs[:, DV:], state), state)
        sin_ref[0] = state
        attn = part_ref[head] + mm(resp_ref[head], state)
        attn_ref[...] = attn
        scale = lax.rsqrt(jnp.mean(attn * attn, axis=-1, keepdims=True) + 1e-05)
        gated = (attn * scale * gain_ref[...] * (gate * jax.nn.sigmoid(gate))).astype(BF16)
        gated_ref[...] = gated

        @pl.when(head == 0)
        def _():
            y_ref[...] = xs_ref[...].astype(F32)

        y_ref[...] += mm(gated, wb_ref[slot, 1], NT)

        @pl.when(head == H - 1)
        def _():
            keep(4).start()
            value = y_ref[...]
            size = lax.rsqrt(jnp.mean(value * value, axis=-1, keepdims=True) + 1e-06)
            mid_ref[...] = (value * size * gains_out[1:2, :]).astype(BF16)
            keep(5).start()
            gathering.finish()

            @pl.when(place < SPOTS - 1)
            def _():
                give_halo().wait_send()

            for which in range(6):
                keep(which).wait()


def mixer_forward(x, cotangent, shards, gains, gain, taps, par, near, later):
    tokens, width = x.shape
    rows = tokens + HALO
    chunks = tokens // CHUNK
    inner = shards[-1].shape[0]
    spans = gather_spans(inner)
    total = AT_FFN + 3 * inner
    once = lambda array: pl.BlockSpec(
        array.shape, lambda s: (0,) * array.ndim, pipeline_mode=pl.Buffered(1)
    )
    whole = lambda shape: pl.BlockSpec(shape, lambda s: (0,) * len(shape))
    early = lambda s: jnp.minimum(s, H - 1)
    late = lambda s: jnp.maximum(s - H, 0)
    by_head = lambda shape, at: pl.BlockSpec(shape, lambda s: (at(s),) + (0,) * (len(shape) - 1))
    across = lambda shape, at: pl.BlockSpec(shape, lambda s: (0, at(s)))
    anywhere = pl.BlockSpec(memory_space=pl.ANY)
    shape = jax.ShapeDtypeStruct
    sem = pltpu.SemaphoreType.DMA
    saved = saved_shapes(chunks)
    return pl.pallas_call(
        functools.partial(mixer_forward_kernel, spans=spans, inner=inner),
        grid=(2 * H,),
        in_specs=[once(a) for a in (x, cotangent, *shards, gains, gain)]
        + [across((8, HC), early)]
        + [once(a) for a in (par, near, later)],
        out_specs=[anywhere] * 7
        + [
            whole((8, width)),
            whole((tokens, LANES)),
            whole((rows, LANES)),
            across((rows, HC), early),
            whole((rows, LANES)),
            across((tokens, DK), early),
        ]
        + [by_head((1,) + one.shape[1:], early) for one in saved]
        + [
            pl.BlockSpec((2, 1, DK, DK), lambda s: (0, late(s), 0, 0)),
            by_head((1, DK, DV), late),
            across((tokens, DV), late),
            across((tokens, DV), late),
            across((tokens, DV), late),
        ],
        out_shape=[
            shape((width, total), BF16),
            shape((rows, width), BF16),
            shape((tokens, width), BF16),
            shape((tokens, width), BF16),
            shape((width, width), BF16),
            shape((tokens, width), F32),
            shape((tokens, width), BF16),
            shape((8, width), F32),
            shape((tokens, LANES), F32),
            shape((rows, LANES), F32),
            shape((rows, H * HC), BF16),
            shape((rows, LANES), F32),
            shape((tokens, H * DK), BF16),
        ]
        + saved
        + [
            shape((2, H, DK, DK), BF16),
            shape((H, DK, DV), F32),
            shape((tokens, H * DV), F32),
            shape((tokens, H * DV), F32),
            shape((tokens, H * DV), BF16),
        ],
        scratch_shapes=[
            pltpu.VMEM((shards[0].shape[0], total), BF16),
            pltpu.VMEM((rows, width), BF16),
            pltpu.VMEM((tokens, width), BF16),
            pltpu.VMEM((tokens, width), BF16),
            pltpu.VMEM((width, width), BF16),
            pltpu.VMEM((tokens, width), F32),
            pltpu.VMEM((tokens, width), BF16),
            pltpu.VMEM((HALO, width), BF16),
            pltpu.VMEM((H, tokens, DV), F32),
            pltpu.VMEM((H, tokens, DK), BF16),
            pltpu.VMEM((H, DK, DV + DK), BF16),
            pltpu.VMEM((H, DK, DV + DK), BF16),
            pltpu.VMEM((H, DK, DV), BF16),
            pltpu.VMEM((H, DK, DV), BF16),
            pltpu.VMEM((tokens, LANES), F32),
            pltpu.VMEM((tokens, LANES), F32),
            pltpu.VMEM((tokens, LANES), F32),
            pltpu.VMEM((rows, HC), F32),
            pltpu.VMEM((tokens, HC), F32),
            pltpu.VMEM((width, HC), BF16),
            pltpu.VMEM((width, LANES), BF16),
            pltpu.VMEM((2, 2, width, DV), BF16),
            sem((len(spans), 10)),
            sem((len(spans), 7)),
            sem((len(spans), SPOTS)),
            sem((2, H)),
            sem((2, H)),
            sem((2,)),
            sem((2, 2)),
            sem((6,)),
            sem((2,)),
        ],
        compiler_params=params(collective_id=0, has_side_effects=True),
        cost_estimate=cost(1e11, 1e8),
        name="mixer_forward",
    )(x, cotangent, *shards, gains, gain, taps, par, near, later)


def backward_kernel(place_ref, slot_ref, *refs):
    exch_ref, grads_ref, refs = refs[9], refs[10], refs[:9] + refs[11:]

    def behind(source, grad):
        slot = slot_ref[source]
        return jnp.where(
            source > place_ref[0],
            grads_ref[slot, 0].astype(F32) + mm(exch_ref[slot, 0], grad, TN),
            grad,
        )

    places = exch_ref.shape[0]
    d_state = lax.fori_loop(
        0, places - 1, lambda lap, grad: behind(places - 1 - lap, grad), jnp.zeros((DK, DV), F32)
    )
    backward_head(pl.program_id(0), d_state, *refs)


def backward_head(
    head, d_state, p_ref, taps_ref, logit_ref, par_ref, cols_ref, back_ref, segr_ref,
    dattn_ref, sin_ref,
    inv_ref, upd_ref, st_ref, stm_ref, amap_ref, rmap_ref,
    dp_ref, dlogit_ref, dtaps_ref, dpar_ref,
    beta_ref, decay_ref, cum_ref, pf_ref, pre_ref, dmix_ref,
):
    @pl.when(head == 0)
    def _():
        gate_tables(logit_ref, par_ref, beta_ref, decay_ref, cum_ref)
        dlogit_ref[...] = jnp.zeros_like(dlogit_ref)
        dpar_ref[...] = jnp.zeros_like(dpar_ref)

    cols = cols_ref[...]
    tokens = cols.shape[0]
    chunks = range(tokens // CHUNK)
    pre = mix_taps(p_ref, taps_ref, cols, pf_ref)
    pre_ref[...] = pre
    beta = lane(beta_ref[...], head + H)

    state_in = sin_ref[0]
    d_states = [None] * len(chunks)
    for c in reversed(chunks):
        rows = slice(c * CHUNK, (c + 1) * CHUNK)
        d_states[c] = d_state
        if c > 0:
            d_state = mm(amap_ref[0, c], d_state, TN) + mm(rmap_ref[0, c], dattn_ref[rows, :], TN)

    row_ids, col_ids = iota2((CHUNK, CHUNK), 0), iota2((CHUNK, CHUNK), 1)
    d_beta_all, d_decay_all = [], []
    for c in chunks:
        rows = slice(c * CHUNK, (c + 1) * CHUNK)
        mixed = pre_ref[rows, :]
        gate = jax.nn.sigmoid(mixed)
        slope = gate * (1.0 + mixed * (1.0 - gate))
        mixed = mixed * gate
        query_raw, key_raw, value = mixed[:, :DK], mixed[:, DK : 2 * DK], mixed[:, 2 * DK :]
        query_size = lax.rsqrt(jnp.sum(query_raw * query_raw, axis=1, keepdims=True) + 1e-06)
        key_size = lax.rsqrt(jnp.sum(key_raw * key_raw, axis=1, keepdims=True) + 1e-06)
        query_unit, key = query_raw * query_size, key_raw * key_size
        query = query_unit * DK**-0.5
        gamma, strict, carry, last = chunk_tables(c, head, cols, segr_ref, cum_ref)
        strength = beta[rows]
        dots = mm(jnp.concatenate([key, query], axis=0), key, NT)
        weights = strict * dots[:CHUNK]
        low = strength * weights
        scores = gamma * dots[CHUNK:]
        if c == 0:
            state = state_in
        else:
            state = st_ref[0, c] + mm(stm_ref[0, c], state_in)
        updates = upd_ref[0, rows, :DV] - mm(upd_ref[0, rows, DV:], state)
        d_attn = dattn_ref[rows, :]
        d_state = d_states[c]
        d_updates = mm(scores, d_attn, TN) + mm(last * key, d_state)
        solved = mm(inv_ref[0, c], d_updates, TN)
        both = jnp.concatenate([d_attn, solved.astype(BF16)], axis=0)
        by_updates = mm(both, updates, NT)
        by_state = mm(both, state, NT)
        d_scores = by_updates[:CHUNK]
        d_low = -by_updates[CHUNK:]
        d_query = carry * by_state[:CHUNK]
        key_state = jnp.sum(key * by_state[CHUNK:], axis=1, keepdims=True)
        d_carry = jnp.sum(query * by_state[:CHUNK], axis=1, keepdims=True) - strength * key_state
        d_beta = (
            jnp.sum(solved * value, axis=1, keepdims=True)
            - carry * key_state
            + jnp.sum(d_low * weights, axis=1, keepdims=True)
        )
        d_dots_q = d_scores * gamma
        d_dots_k = d_low * strength * strict
        by_key = mm(jnp.concatenate([d_dots_q, d_dots_k], axis=0), key)
        d_query += by_key[:CHUNK]
        from_state = mm(updates, d_state, NT)
        d_key = (
            by_key[CHUNK:]
            + mm(
                jnp.concatenate([d_dots_q, d_dots_k], axis=0),
                jnp.concatenate([query, key], axis=0),
                TN,
            )
            - strength * carry * by_state[CHUNK:]
            + last * from_state
        )
        d_last = jnp.sum(key * from_state, axis=1, keepdims=True) * last
        d_spread = d_scores * scores + d_low * low
        final = (iota2((CHUNK, 1), 0) == CHUNK - 1).astype(F32)
        d_carry += final * jnp.sum(d_state * state)
        d_cum = (
            jnp.sum(d_spread, axis=1, keepdims=True)
            - to_column(jnp.sum(d_spread, axis=0, keepdims=True))
            + final * jnp.sum(d_last)
            - d_last
            + d_carry * carry
        )
        d_decay = jnp.sum(
            jnp.where(row_ids <= col_ids, to_row(d_cum), 0.0), axis=1, keepdims=True
        )
        d_beta_all.append(d_beta)
        d_decay_all.append(d_decay)
        d_query = d_query * DK**-0.5
        d_query = query_size * (
            d_query - query_unit * jnp.sum(d_query * query_unit, axis=1, keepdims=True)
        )
        d_key = key_size * (d_key - key * jnp.sum(d_key * key, axis=1, keepdims=True))
        d_value = strength * solved
        dmix_ref[HALO + c * CHUNK : HALO + (c + 1) * CHUNK, :] = slope * jnp.concatenate(
            [d_query, d_key, d_value], axis=1
        )

    d_beta = jnp.concatenate(d_beta_all, axis=0)
    d_decay = jnp.concatenate(d_decay_all, axis=0)
    lanes = iota2((tokens, LANES), 1)
    slope = jax.nn.sigmoid(logit_ref[HALO:, :] + par_ref[1:2, :]) * -jnp.exp(par_ref[0:1, :])
    here = jnp.where(lanes == head, d_decay, 0.0)
    d_first = here * slope
    strengths = beta_ref[...]
    d_second = jnp.where(lanes == head + H, d_beta, 0.0) * strengths * (1.0 - strengths)
    dlogit_ref[...] += d_first + d_second
    dpar_ref[0:1, :] += jnp.sum(here * decay_ref[...], axis=0, keepdims=True)
    dpar_ref[1:2, :] += jnp.sum(d_first, axis=0, keepdims=True)

    dmix_ref[:HALO, :] = jnp.zeros((HALO, HC), F32)
    dmix_ref[HALO + tokens :, :] = jnp.zeros((8, HC), F32)
    d_mix = dmix_ref[HALO : HALO + tokens, :]
    dtaps_ref[...] = jnp.zeros_like(dtaps_ref)
    dtaps_ref[0:1, :] = jnp.sum(d_mix * pf_ref[HALO:, :], axis=0, keepdims=True)
    total = dmix_ref[: HALO + tokens, :] * taps_ref[0:1, :]
    for j in range(1, CONV):
        total += dmix_ref[j : j + HALO + tokens, :] * taps_ref[j : j + 1, :] * back_ref[:, j : j + 1]
        dtaps_ref[j : j + 1, :] = jnp.sum(
            d_mix * cols[:, j : j + 1] * pf_ref[HALO - j : HALO - j + tokens, :],
            axis=0,
            keepdims=True,
        )
    dp_ref[...] = total.astype(BF16)


def delta_backward(
    place, slots, proj, taps, logits, par, cols, back, segr, d_attn, state_in, exch, grads, saved
):
    rows = proj.shape[0]
    tokens = rows - HALO
    chunks = tokens // CHUNK
    places = exch.shape[0]
    whole = lambda shape: pl.BlockSpec(shape, lambda h: (0,) * len(shape))
    by_head = lambda shape: pl.BlockSpec(shape, lambda h: (h,) + (0,) * (len(shape) - 1))
    return pl.pallas_call(
        backward_kernel,
        grid=(H,),
        in_specs=[
            pl.BlockSpec(memory_space=pltpu.SMEM),
            pl.BlockSpec(memory_space=pltpu.SMEM),
            pl.BlockSpec((rows, HC), lambda h: (0, h)),
            pl.BlockSpec((8, HC), lambda h: (0, h)),
            whole((rows, LANES)),
            whole((8, LANES)),
            whole((tokens, LANES)),
            whole((rows, LANES)),
            whole(segr.shape),
            pl.BlockSpec((tokens, DV), lambda h: (0, h)),
            by_head((1, DK, DV)),
            pl.BlockSpec((places, 1, DK, DK), lambda h: (0, h, 0, DV // DK)),
            pl.BlockSpec((places, 1, DK, DV), lambda h: (0, h, 0, 0)),
            by_head((1, chunks, CHUNK, CHUNK)),
            by_head((1, tokens, DV + DK)),
            by_head((1, chunks, DK, DV)),
            by_head((1, chunks, DK, DK)),
            by_head((1, chunks, DK, DK)),
            by_head((1, chunks, CHUNK, DK)),
        ],
        out_specs=[
            pl.BlockSpec((rows, HC), lambda h: (0, h)),
            whole((tokens, LANES)),
            pl.BlockSpec((8, HC), lambda h: (0, h)),
            whole((8, LANES)),
        ],
        out_shape=[
            jax.ShapeDtypeStruct((rows, H * HC), BF16),
            jax.ShapeDtypeStruct((tokens, LANES), F32),
            jax.ShapeDtypeStruct((8, H * HC), F32),
            jax.ShapeDtypeStruct((8, LANES), F32),
        ],
        scratch_shapes=[
            pltpu.VMEM((tokens, LANES), F32),
            pltpu.VMEM((tokens, LANES), F32),
            pltpu.VMEM((tokens, LANES), F32),
            pltpu.VMEM((rows, HC), F32),
            pltpu.VMEM((tokens, HC), F32),
            pltpu.VMEM((rows + 8, HC), F32),
        ],
        compiler_params=params(),
        cost_estimate=cost(8e9 * H, 5e6 * H),
        name="delta_backward",
    )(place, slots, proj, taps, logits, par, cols, back, segr, d_attn, state_in, exch, grads, *saved)


def mixer_kernel(
    place_ref, slot_ref, part_ref, resp_ref, exch_ref, gpre_ref, gain_ref, w_ref, x_ref, gain2_ref,
    sin_ref, attn_ref, gated_ref, y_ref, h_ref,
):
    head = pl.program_id(0)
    place = place_ref[0]
    places = exch_ref.shape[0]

    def ahead(source, state):
        slot = slot_ref[source]
        return jnp.where(
            source < place,
            exch_ref[slot, 0, :, :DV].astype(F32) + mm(exch_ref[slot, 0, :, DV:], state),
            state,
        )

    state = lax.fori_loop(0, places - 1, ahead, jnp.zeros((DK, DV), F32))
    sin_ref[0] = state
    attn = part_ref[...] + mm(resp_ref[...], state)
    attn_ref[...] = attn
    scale = lax.rsqrt(jnp.mean(attn * attn, axis=-1, keepdims=True) + 1e-05)
    gate = gpre_ref[...]
    gated = (attn * scale * gain_ref[...] * (gate * jax.nn.sigmoid(gate))).astype(BF16)
    gated_ref[...] = gated

    @pl.when(head == 0)
    def _():
        y_ref[...] = x_ref[...].astype(F32)

    y_ref[...] += mm(gated, w_ref[...], NT)

    @pl.when(head == pl.num_programs(0) - 1)
    def _():
        value = y_ref[...]
        size = lax.rsqrt(jnp.mean(value * value, axis=-1, keepdims=True) + 1e-06)
        h_ref[...] = (value * size * gain2_ref[...]).astype(BF16)


def mixer_out(place, slots, part, resp, exch, gpre, gain, weights, x, gain2):
    tokens, width = x.shape
    places = exch.shape[0]
    whole = lambda shape: pl.BlockSpec(shape, lambda h: (0,) * len(shape))
    return pl.pallas_call(
        mixer_kernel,
        grid=(H,),
        in_specs=[
            pl.BlockSpec(memory_space=pltpu.SMEM),
            pl.BlockSpec(memory_space=pltpu.SMEM),
            pl.BlockSpec((tokens, DV), lambda h: (0, h)),
            pl.BlockSpec((tokens, DK), lambda h: (0, h)),
            pl.BlockSpec((places, 1, DK, DV + DK), lambda h: (0, h, 0, 0)),
            pl.BlockSpec((tokens, DV), lambda h: (0, h)),
            whole((1, DV)),
            pl.BlockSpec((width, DV), lambda h: (0, h + AT_OUT // DV)),
            whole((tokens, width)),
            whole((1, width)),
        ],
        out_specs=[
            pl.BlockSpec((1, DK, DV), lambda h: (h, 0, 0)),
            pl.BlockSpec((tokens, DV), lambda h: (0, h)),
            pl.BlockSpec((tokens, DV), lambda h: (0, h)),
            whole((tokens, width)),
            whole((tokens, width)),
        ],
        out_shape=[
            jax.ShapeDtypeStruct((H, DK, DV), F32),
            jax.ShapeDtypeStruct((tokens, H * DV), F32),
            jax.ShapeDtypeStruct((tokens, H * DV), BF16),
            jax.ShapeDtypeStruct((tokens, width), F32),
            jax.ShapeDtypeStruct((tokens, width), BF16),
        ],
        compiler_params=params(),
        cost_estimate=cost(2 * tokens * width * H * DV, 2e7),
        name="mixer_out",
    )(place, slots, part, resp, exch, gpre, gain, weights, x, gain2)


def mixer_back_kernel(
    dmix_ref, w_ref, attn_ref, gpre_ref, gain_ref, resp_ref,
    dattn_ref, dgpre_ref, grad_ref, dgain_ref,
):
    @pl.when(pl.program_id(0) == 0)
    def _():
        dgain_ref[...] = jnp.zeros_like(dgain_ref)

    d_gain, dattn_ref[...], dgpre_ref[...], grad_ref[0] = mixer_back_head(
        dmix_ref, w_ref, attn_ref, gpre_ref, gain_ref, resp_ref
    )
    dgain_ref[0:1, :] += d_gain


def mixer_back_head(dmix_ref, w_ref, attn_ref, gpre_ref, gain_ref, resp_ref):
    d_gated = mm(dmix_ref[...], w_ref[...])
    attn = attn_ref[...]
    size = lax.rsqrt(jnp.mean(attn * attn, axis=-1, keepdims=True) + 1e-05)
    unit = attn * size
    gate = gpre_ref[...]
    slope = jax.nn.sigmoid(gate)
    swish = gate * slope
    gain = gain_ref[...]
    d_gpre = (d_gated * (unit * gain) * (slope * (1.0 + gate * (1.0 - slope)))).astype(BF16)
    d_normed = d_gated * swish
    d_gain = jnp.sum(d_normed * unit, axis=0, keepdims=True)
    d_unit = d_normed * gain
    d_attn = size * (d_unit - unit * jnp.mean(d_unit * unit, axis=-1, keepdims=True))
    d_attn = d_attn.astype(BF16)
    return d_gain, d_attn, d_gpre, mm(resp_ref[...], d_attn, TN).astype(BF16)


def mixer_back(d_mixer, weights, attn, gpre, gain, resp):
    tokens, width = d_mixer.shape
    whole = lambda shape: pl.BlockSpec(shape, lambda h: (0,) * len(shape))
    return pl.pallas_call(
        mixer_back_kernel,
        grid=(H,),
        in_specs=[
            whole((tokens, width)),
            pl.BlockSpec((width, DV), lambda h: (0, h + AT_OUT // DV)),
            pl.BlockSpec((tokens, DV), lambda h: (0, h)),
            pl.BlockSpec((tokens, DV), lambda h: (0, h)),
            whole((1, DV)),
            pl.BlockSpec((tokens, DK), lambda h: (0, h)),
        ],
        out_specs=[
            pl.BlockSpec((tokens, DV), lambda h: (0, h)),
            pl.BlockSpec((tokens, DV), lambda h: (0, h)),
            pl.BlockSpec((1, DK, DV), lambda h: (h, 0, 0)),
            whole((8, DV)),
        ],
        out_shape=[
            jax.ShapeDtypeStruct((tokens, H * DV), BF16),
            jax.ShapeDtypeStruct((tokens, H * DV), BF16),
            jax.ShapeDtypeStruct((H, DK, DV), BF16),
            jax.ShapeDtypeStruct((8, DV), F32),
        ],
        compiler_params=params(),
        cost_estimate=cost(2 * tokens * width * H * DV, 2e7),
        name="mixer_back",
    )(d_mixer, weights, attn, gpre, gain, resp)


def ffn_kernel(
    h_ref, dout_ref, y_ref, gain_ref, turn_ref, wg_ref, wu_ref, wd_ref,
    out_ref, act_ref, dgu_ref, dy_ref, dmix_ref, dgain_ref, res_ref, dh_ref,
):
    step = pl.program_id(0)

    @pl.when(step == 0)
    def _():
        res_ref[...] = y_ref[...]
        dh_ref[...] = jnp.zeros_like(dh_ref)

    hidden = h_ref[...]
    w_gate, w_up, w_down = wg_ref[...], wu_ref[...], wd_ref[...]
    gate = mm(hidden, w_gate)
    up = mm(hidden, w_up)
    d_act = mm(dout_ref[...], w_down)
    slope = jax.nn.sigmoid(gate)
    swish = gate * slope
    act = (swish * up).astype(BF16)
    act_ref[...] = act
    d_gate = (d_act * up * slope * (1.0 + gate * (1.0 - slope))).astype(BF16)
    d_up = (d_act * swish).astype(BF16)
    dgu_ref[0] = d_gate
    dgu_ref[1] = d_up
    res_ref[...] += mm(act, w_down, NT)
    dh_ref[...] += mm(d_gate, w_gate, NT) + mm(d_up, w_up, NT)

    @pl.when(step == pl.num_programs(0) - 1)
    def _():
        out_ref[...] = mm(res_ref[...], turn_ref[...], NT).astype(BF16)
        value = y_ref[...]
        size = lax.rsqrt(jnp.mean(value * value, axis=-1, keepdims=True) + 1e-06)
        unit = value * size
        d_hidden = dh_ref[...]
        dgain_ref[...] = jnp.zeros_like(dgain_ref)
        dgain_ref[0:1, :] = jnp.sum(d_hidden * unit, axis=0, keepdims=True)
        d_unit = d_hidden * gain_ref[...]
        d_y = dout_ref[...].astype(F32) + size * (
            d_unit - unit * jnp.mean(d_unit * unit, axis=-1, keepdims=True)
        )
        dy_ref[...] = d_y
        dmix_ref[...] = d_y.astype(BF16)


def feed_forward(hidden, d_out, y1, gain, turn, weights, inner):
    tokens, width = hidden.shape
    block = 256
    weight = lambda at: pl.BlockSpec((width, block), lambda j: (0, j + at // block))
    whole = lambda shape: pl.BlockSpec(shape, lambda j: (0,) * len(shape))
    across = pl.BlockSpec((tokens, block), lambda j: (0, j))
    return pl.pallas_call(
        ffn_kernel,
        grid=(inner // block,),
        in_specs=[
            whole((tokens, width)),
            whole((tokens, width)),
            whole((tokens, width)),
            whole((1, width)),
            pl.BlockSpec((width, width), lambda j: (0, 0), pipeline_mode=pl.Buffered(1)),
        ]
        + [weight(AT_FFN + i * inner) for i in range(3)],
        out_specs=[
            whole((tokens, width)), across, pl.BlockSpec((2, tokens, block), lambda j: (0, 0, j)),
            whole((tokens, width)), whole((tokens, width)), whole((8, width)),
        ],
        out_shape=[
            jax.ShapeDtypeStruct((tokens, width), BF16),
            jax.ShapeDtypeStruct((tokens, inner), BF16),
            jax.ShapeDtypeStruct((2, tokens, inner), BF16),
            jax.ShapeDtypeStruct((tokens, width), F32),
            jax.ShapeDtypeStruct((tokens, width), BF16),
            jax.ShapeDtypeStruct((8, width), F32),
        ],
        scratch_shapes=[pltpu.VMEM((tokens, width), F32), pltpu.VMEM((tokens, width), F32)],
        compiler_params=params(),
        cost_estimate=cost(12 * tokens * width * inner, 3e7),
        name="feed_forward",
    )(hidden, d_out, y1, gain, turn, weights, weights, weights)


BLOCK = HC
LEAD, EVERY = 5, 3


def other_index(step):
    return step - jnp.clip((step - LEAD + EVERY - 1) // EVERY, 0, H)


class Blocks:
    def __init__(self, inner):
        self.ups, self.downs = inner // (BLOCK // 2), inner // BLOCK
        self.outs = H * DV // BLOCK
        self.others = self.ups + self.downs + 2 * self.outs
        self.count = self.others + H + 1
        self.starts = [0, self.ups, self.ups + self.downs, self.ups + self.downs + self.outs, self.others]
        self.tail = inner - self.downs * BLOCK
        heads = [LEAD + EVERY * h for h in range(H)]
        rest = [n for n in range(self.count - 1) if n not in heads]
        parts = [rest[low:high] for low, high in zip(self.starts, self.starts[1:])]
        self.up_at, self.down_at, self.out_at, self.gate_at = parts
        self.head_at = heads

    def index(self, kind):
        low, high = self.starts[kind], self.starts[kind + 1]
        return lambda s: jnp.clip(other_index(s) - low, 0, high - low - 1)


def dot_blocks(left, right):
    return lax.dot_general(left, right, (NN, ((), ())), preferred_element_type=F32)


def flip_to(bit):
    here = lax.axis_index("seq")
    along_x = here + 1 - 2 * lax.rem(here, 2)
    along_y = here + 2 - 4 * (here // 2)
    return {"dp": lax.axis_index("dp"), "seq": (2 - bit) * along_x + (bit - 1) * along_y}


def reduce_kernel(
    dout_any, hmid_any, hidden_any, x_any, dy_any, turn_any, dres_ref,
    act_ref, tail_ref, dgu_ref, gated_ref, wout_ref, attn_ref, gpre_ref, gain_ref, resp_ref, win_ref, wl_ref,
    gains_ref, dffn_ref,
    p_ref, taps_ref, logit_ref, par_ref, cols_ref, back_ref, segr_ref, sin_ref, maps_ref,
    inv_ref, upd_ref, st_ref, stm_ref, amap_ref, rmap_ref,
    sum_ref, dx_ref, small_ref,
    dlogit_ref, dtaps_ref, dpar_ref, dgain_ref, dattn_ref, dgpre_ref, lgrad_ref, acc_ref, left_ref,
    total_ref, other_ref,
    beta_ref, decay_ref, cum_ref, pf_ref, pre_ref, dmix_ref,
    turn_ref, dps_ref, halo_ref, grads_ref, halves_ref,
    core_keep, core_send, core_recv, near_keep, near_send, near_recv,
    z_keep, pair_send, pair_recv, cross_send, cross_recv, far_send, far_recv, done_ref,
    core_ss, core_rs, near_ss, near_rs, pair_ss, pair_rs, cross_ss, cross_rs, far_ss, far_rs, done_ss, done_rs, own_sem,
    halo_ss, halo_rs, grads_ss, grads_rs, load_sem, small_ss, small_rs, *, blocks,
):
    step = pl.program_id(0)
    steps = pl.num_programs(0)
    place = lax.axis_index("seq")
    count = blocks.count
    half = core_keep.shape[1] * core_keep.shape[2]
    quarter = half // SPOTS
    piece = quarter // PLANES
    mesh = dict(device_id_type=pl.DeviceIdType.MESH)

    def remote(source, target, send, recv, to):
        return pltpu.make_async_remote_copy(
            src_ref=source, dst_ref=target, send_sem=send, recv_sem=recv, device_id=to, **mesh
        )

    def to_core(n):
        mine, slot = lax.rem(n, 3), lax.rem(n, 4)
        return remote(core_send.at[mine], core_recv.at[slot], core_ss.at[mine], core_rs.at[slot], device(core=1))

    def to_near(n):
        slot = lax.rem(n, 4)
        return remote(
            near_send.at[slot], near_recv.at[slot], near_ss.at[slot], near_rs.at[slot], flip_to(1 + lax.rem(n, 2))
        )

    def to_far(n):
        slot = lax.rem(n, 4)
        return remote(
            far_send.at[slot], far_recv.at[slot], far_ss.at[slot], far_rs.at[slot], flip_to(2 - lax.rem(n, 2))
        )

    z = lax.axis_index("dp") // CORES
    inner = (z > 0) & (z < PLANES - 1)
    outer_plane = (z == 0) | (z == PLANES - 1)

    def to_pair(n, pieces):
        slot = lax.rem(n, 4)
        return remote(
            pair_send.at[slot, 0:pieces], pair_recv.at[slot, 0:pieces], pair_ss.at[slot], pair_rs.at[slot],
            device(planes=1 + 2 * lax.rem(z, 2)),
        )

    def to_cross(n, outside):
        planes = 2 if outside else 2 * z - 1
        slot = lax.rem(n, 4)
        return remote(
            cross_send.at[slot, outside], cross_recv.at[n], cross_ss.at[slot, outside], cross_rs.at[n],
            device(planes=planes),
        )

    def target(n, which):
        spot = place if which == 0 else flip_spot(place, 2 - lax.rem(n, 2))
        return sum_ref.at[
            pl.ds(pl.multiple_of(spot * piece, piece), piece), pl.ds(pl.multiple_of(n * BLOCK, BLOCK), BLOCK)
        ]

    def spread(n, which):
        slot = lax.rem(n, 4)
        return remote(
            done_ref.at[slot, which], target(n, which), done_ss.at[slot, which], done_rs.at[n, which],
            flip_to(1 + lax.rem(n, 2)),
        )

    def keep(n, which):
        slot = lax.rem(n, 4)
        return pltpu.make_async_copy(done_ref.at[slot, which], target(n, which), own_sem.at[slot, which])

    upper = place // 2 == 1
    second = lax.rem(place, 2) == 1

    def give_grads(head):
        return remote(
            lgrad_ref.at[head], grads_ref.at[0, head], grads_ss.at[0, head], grads_rs.at[0, head], device(spot=1)
        )

    def give_half(head):
        return remote(
            halves_ref.at[head], grads_ref.at[1, head], grads_ss.at[1, head], grads_rs.at[1, head], device(spot=2)
        )

    def give_small(stage):
        to = (dict(core=1), dict(spot=1), dict(spot=2), dict(planes=1), dict(planes=2), dict(planes=3))[stage]
        return remote(
            total_ref.at[min(stage, 3)], other_ref.at[stage], small_ss.at[stage], small_rs.at[stage], device(**to)
        )

    def load(at, source, to):
        return pltpu.make_async_copy(source, to, load_sem.at[at])

    def final_loads():
        width = turn_any.shape[0]
        copies = []
        for n in range(2):
            cols = slice(n * (width // 2), (n + 1) * (width // 2))
            copies.append(load(n, turn_any.at[:, cols], turn_ref.at[n]))
            rows = x_any.shape[0]
            copies.append(load(2 + n, x_any.at[:, cols], turn_ref.at[2, n * rows : (n + 1) * rows]))
            for q in range(SPOTS):
                copies.append(
                    load(4 + n * SPOTS + q, dy_any.at[q * quarter : (q + 1) * quarter, cols], core_keep.at[n, q])
                )
        return copies

    def final_stores():
        width = dx_ref.shape[1]
        return [
            load(
                n * SPOTS + q,
                core_keep.at[n, q],
                dx_ref.at[q * quarter : (q + 1) * quarter, n * (width // 2) : (n + 1) * (width // 2)],
            )
            for n in range(2)
            for q in range(SPOTS)
        ]

    def give_halo(head):
        to = {"dp": lax.axis_index("dp"), "seq": lax.rem(place + SPOTS - 1, SPOTS)}
        return remote(dps_ref.at[0:HALO], halo_ref.at[head], halo_ss.at[head], halo_rs.at[head], to)

    @pl.when(step == 0)
    def _():
        greet([dict(planes=d) for d in (1, 2, 3)] + [dict(spot=s) for s in (1, 2, 3)] + [dict(core=1)])
        dgain_ref[...] = jnp.zeros_like(dgain_ref)
        acc_ref[...] = jnp.zeros_like(acc_ref)

    def left(n):
        tokens = dres_ref.shape[0]
        source = (hmid_any, dout_any, hidden_any.at[HALO : HALO + tokens])[n]
        return load(n, source, left_ref.at[n % 2])

    for n, at in enumerate((1, 0, 3, 2)):

        @pl.when(step == n)
        def _(n=n, at=at):
            if n == 0:
                left(0).start()
            if n < 2:
                left(n + 1).start()
            if n < 3:
                left(n).wait()
                turn_ref[at] = jnp.transpose(left_ref[n % 2])
            else:
                turn_ref[at] = jnp.transpose(dres_ref[...])

    def at_stage(lag, sent):
        n = step - lag

        def run(body):
            @pl.when((n >= 0) & (n < count))
            def _():
                @pl.when(n >= sent)
                def _():
                    body(n, True)

                body(n, False)

        return run

    @at_stage(10, 4)
    def _(n, free):
        if free:
            for which in range(2):
                spread(n - 4, which).wait_send()
                keep(n - 4, which).wait()
            return
        slot = lax.rem(n, 4)
        to_far(n).wait_recv()
        for which in range(2):
            total = far_send[slot, which].astype(F32) + far_recv[slot, 1 - which].astype(F32)
            done_ref[slot, which] = total.astype(BF16)
            keep(n, which).start()
            spread(n, which).start()

    @at_stage(8, 4)
    def _(n, free):
        if free:
            to_far(n - 4).wait_send()
            return
        slot = lax.rem(n, 4)
        to_cross(n, 0).wait_recv()
        total = (z_keep[slot, 0] + cross_recv[n].astype(F32)).astype(BF16)
        far_send[slot, 0], far_send[slot, 1] = total[:piece], total[piece:]
        to_far(n).start()

    @at_stage(6, 4)
    def _(n, free):
        slot = lax.rem(n, 4)
        if free:

            @pl.when(inner)
            def _():
                to_cross(n - 4, 0).wait_send()
                to_cross(n - 4, 1).wait_send()

            return

        @pl.when(outer_plane)
        def _():
            to_pair(n, 1).wait_recv()

        @pl.when(inner)
        def _():
            to_pair(n, 3).wait_recv()
            for outside, at in enumerate((5 - 2 * z, 2)):
                cross_send[slot, outside] = (
                    z_keep[slot, at] + pair_recv[slot, 1 + outside].astype(F32)
                ).astype(BF16)
                to_cross(n, outside).start()

        z_keep[slot, 0] += pair_recv[slot, 0].astype(F32)

    @at_stage(4, 4)
    def _(n, free):
        slot = lax.rem(n, 4)
        if free:

            @pl.when(outer_plane)
            def _():
                to_pair(n - 4, 3).wait_send()

            @pl.when(inner)
            def _():
                to_pair(n - 4, 1).wait_send()

            return
        to_near(n).wait_recv()
        for which in range(2):
            total = near_keep[slot, which] + near_recv[slot, which].astype(F32)
            for d in range(PLANES):
                z_keep[slot, d, which * piece : (which + 1) * piece] = total[d * piece : (d + 1) * piece]

        @pl.when(outer_plane)
        def _():
            up = 1 - z // 3
            for k in range(3):
                pair_send[slot, k] = z_keep[slot, up * (3 - k) + (1 - up) * (1 + k)].astype(BF16)
            to_pair(n, 3).start()

        @pl.when(inner)
        def _():
            pair_send[slot, 0] = z_keep[slot, 2 * z - 1].astype(BF16)
            to_pair(n, 1).start()

    @at_stage(2, 4)
    def _(n, free):
        if free:
            to_near(n - 4).wait_send()
            return
        slot, mine = lax.rem(n, 4), lax.rem(n, 3)
        first = 1 + lax.rem(n, 2)
        to_core(n).wait_recv()
        whole = lambda quarter: core_keep[mine, quarter] + core_recv[slot, quarter].astype(F32)
        near_keep[slot, 0] = whole(0)
        near_keep[slot, 1] = whole(3 - first)
        near_send[slot, 0] = whole(first).astype(BF16)
        near_send[slot, 1] = whole(3).astype(BF16)
        to_near(n).start()

    since = step - LEAD
    heads_turn = (since >= 0) & (since < EVERY * H) & (lax.rem(jnp.maximum(since, 0), EVERY) == 0)
    other = other_index(step)

    def put(product):
        mine = lax.rem(step, 3)

        @pl.when(step >= 3)
        def _():
            to_core(step - 3).wait_send()

        for q in range(SPOTS):
            core_keep[mine, q] = product[q * quarter : (q + 1) * quarter]
            core_send[mine, q] = product[half + q * quarter : half + (q + 1) * quarter].astype(BF16)
        to_core(step).start()

    def on(kind):
        low, high = blocks.starts[kind], blocks.starts[kind + 1]
        return pl.when((other >= low) & (other < high) & jnp.logical_not(heads_turn))

    @on(0)
    def _():
        put(dot_blocks(turn_ref[1], jnp.concatenate([dgu_ref[0], dgu_ref[1]], axis=1)))

    @on(1)
    def _():
        put(dot_blocks(turn_ref[0], act_ref[...]))

    @on(2)
    def _():
        put(dot_blocks(turn_ref[2], gated_ref[...]))

    @on(3)
    def _():
        gate = other - blocks.starts[3]
        value = jnp.concatenate([dgpre_ref[2 * gate], dgpre_ref[2 * gate + 1]], axis=1)
        acc_ref[...] += mm(value, win_ref[...], NT)
        put(dot_blocks(turn_ref[3], value))

    @pl.when(step == count - 1)
    def _():
        down = dot_blocks(turn_ref[0], tail_ref[...])
        gates = dot_blocks(turn_ref[3], dlogit_ref[...].astype(BF16))
        acc_ref[...] += mm(dlogit_ref[...], wl_ref[...], NT)
        rest = jnp.zeros((down.shape[0], BLOCK - down.shape[1] - LANES), F32)
        put(jnp.concatenate([down, gates, rest], axis=1))

    @pl.when(heads_turn)
    def _():
        head = since // EVERY

        @pl.when(place > 0)
        def _():
            give_halo(head).wait_send()

        @pl.when(place < SPOTS - 1)
        def _():
            give_halo(head).wait_recv()
            tokens = dps_ref.shape[0] - HALO
            dps_ref[tokens:, :] = (
                dps_ref[tokens:, :].astype(F32) + halo_ref[head].astype(F32)
            ).astype(BF16)

        value = dps_ref[HALO:, :]
        acc_ref[...] += mm(value, win_ref[...], NT)
        put(dot_blocks(turn_ref[3], value))

    @pl.when(step < H)
    def _():
        d_gain, dattn_ref[step], dgpre_ref[step], lgrad_ref[step] = mixer_back_head(
            dres_ref, wout_ref, attn_ref, gpre_ref, gain_ref, resp_ref
        )
        dgain_ref[...] += d_gain
        give_grads(step).start()

    @pl.when((step >= 2) & (step < H + 2))
    def _():
        head = step - 2
        give_grads(head).wait()

        @pl.when(upper)
        def _():
            mine, theirs = lgrad_ref[head], grads_ref[0, head]
            earlier = jnp.where(second, theirs, mine)
            later = jnp.where(second, mine, theirs)
            through = jnp.where(second, maps_ref[1, head], maps_ref[0, head])
            halves_ref[head] = (earlier.astype(F32) + mm(through, later, TN)).astype(BF16)
            give_half(head).start()

    @pl.when((since >= -1) & (since < EVERY * H - 1) & (lax.rem(jnp.maximum(since + 1, 0), EVERY) == 0))
    def _():
        head = (since + 1) // EVERY

        @pl.when(upper)
        def _():
            grads_ref[1, head] = jnp.zeros((DK, DV), BF16)
            give_half(head).wait_send()

        @pl.when(jnp.logical_not(upper))
        def _():
            give_half(head).wait_recv()

        d_state = grads_ref[1, head].astype(F32)
        nearer = grads_ref[0, head].astype(F32) + mm(maps_ref[1, head], d_state, TN)
        d_state = jnp.where(second, d_state, nearer)
        backward_head(
            head, d_state, p_ref, taps_ref, logit_ref, par_ref, cols_ref, back_ref, segr_ref,
            dattn_ref.at[head], sin_ref, inv_ref, upd_ref, st_ref, stm_ref, amap_ref, rmap_ref,
            dps_ref, dlogit_ref, dtaps_ref, dpar_ref, beta_ref, decay_ref, cum_ref, pf_ref, pre_ref, dmix_ref,
        )
        total_ref[0, pl.ds(pl.multiple_of(head * 8, 8), 8), :] = dtaps_ref[...]

        @pl.when(place > 0)
        def _():
            give_halo(head).start()

    @pl.when(step == count)
    def _():
        for copy in final_loads():
            copy.start()

    @pl.when(step == count + 2)
    def _():
        for copy in final_loads():
            copy.wait()
        tokens, width = acc_ref.shape
        middle = width // 2
        halves_of = lambda ref: jnp.concatenate([ref[0], ref[1]], axis=1)
        value = jnp.concatenate([turn_ref[2, :tokens], turn_ref[2, tokens:]], axis=1).astype(F32)
        size = lax.rsqrt(jnp.mean(value * value, axis=-1, keepdims=True) + 1e-06)
        unit = value * size
        d_hidden = acc_ref[...]
        d_gain = jnp.sum(d_hidden * unit, axis=0, keepdims=True)
        d_unit = d_hidden * gains_ref[0:1, :]
        through = size * (d_unit - unit * jnp.mean(d_unit * unit, axis=-1, keepdims=True))
        d_y = [jnp.concatenate([core_keep[n, q] for q in range(SPOTS)], axis=0) for n in range(2)]
        total = jnp.concatenate(d_y, axis=1) + through

        def natural(part):
            return mm(part[:, :middle], turn_ref[0], NT) + mm(part[:, middle:], turn_ref[1], NT)

        high, low = halves(total)
        total = natural(high) + natural(low)
        for n in range(2):
            for q in range(SPOTS):
                core_keep[n, q] = total[q * quarter : (q + 1) * quarter, n * middle : (n + 1) * middle]
        for copy in final_stores():
            copy.start()
        gains = jnp.concatenate([d_gain, dffn_ref[0:1, :], jnp.zeros((6, width), F32)], axis=0)
        high, mid = halves(gains)
        gains = natural(high) + natural(mid) + natural((gains - high.astype(F32)) - mid.astype(F32))
        base = 8 * H
        total_ref[0, base : base + 8, :] = gains[:, :middle]
        total_ref[0, base + 8 : base + 16, :] = gains[:, middle:]
        total_ref[0, base + 16 : base + 24, : dgain_ref.shape[1]] = dgain_ref[...]
        total_ref[0, base + 16 : base + 24, dgain_ref.shape[1] : dgain_ref.shape[1] + LANES] = dpar_ref[...]
        total_ref[0, base + 16 : base + 24, dgain_ref.shape[1] + LANES :] = jnp.zeros((8, LANES), F32)
        give_small(0).start()

    for stage in range(3):

        @pl.when(step == count + 3 + stage)
        def _(stage=stage):
            give_small(stage).wait_recv()
            total_ref[stage + 1] = total_ref[stage] + other_ref[stage]
            for later in (stage + 1,) if stage < 2 else (3, 4, 5):
                give_small(later).start()

    @pl.when(step == count + 6)
    def _():
        total = total_ref[3]
        for stage in (3, 4, 5):
            give_small(stage).wait_recv()
            total += other_ref[stage]
        small_ref[...] = total
        for stage in range(6):
            give_small(stage).wait_send()
        for copy in final_stores():
            copy.wait()

    @pl.when(step == steps - 1)
    def _():
        for n in range(count - 4, count):
            if n >= count - 3:
                to_core(n).wait_send()
            to_near(n).wait_send()
            to_far(n).wait_send()

            @pl.when(outer_plane)
            def _(n=n):
                to_pair(n, 3).wait_send()

            @pl.when(inner)
            def _(n=n):
                to_pair(n, 1).wait_send()
                to_cross(n, 0).wait_send()
                to_cross(n, 1).wait_send()

            for which in range(2):
                spread(n, which).wait_send()
                keep(n, which).wait()

        def arrived(n, carry):
            for which in range(2):
                spread(n, which).wait_recv()
            return carry

        lax.fori_loop(0, count, arrived, 0)


def reduce_gradients(
    d_out, hidden_mid, hidden, x, d_y, turn, d_mixer, act, d_gu, gated, weights, attn, gpre, gain_out, resp, gains,
    d_ffn, proj, taps, logits, par, cols, back, segr, state_in, maps, saved,
):
    tokens, width = d_mixer.shape
    rows = hidden.shape[0]
    chunks = tokens // CHUNK
    blocks = Blocks(act.shape[1])
    half = width // CORES
    quarter = half // SPOTS
    piece = quarter // PLANES
    small = 8 * H + 24
    anywhere = pl.BlockSpec(memory_space=pl.ANY)
    whole = lambda shape: pl.BlockSpec(shape, lambda s: (0,) * len(shape))
    once = lambda shape: pl.BlockSpec(shape, lambda s: (0,) * len(shape), pipeline_mode=pl.Buffered(1))
    coming = lambda s: jnp.clip((s + EVERY - LEAD) // EVERY, 0, H - 1)
    starting = lambda s: jnp.minimum(s, H - 1)
    by_head = lambda shape: pl.BlockSpec(shape, lambda s: (coming(s),) + (0,) * (len(shape) - 1))
    across = lambda shape, at: pl.BlockSpec(shape, lambda s: (0, at(s)))
    sem = pltpu.SemaphoreType.DMA
    up, down, out, gate = (blocks.index(kind) for kind in range(4))
    first_gate = blocks.gate_at[0]

    def win(s):
        no_head = ((s - LEAD) % EVERY != 0) | (s > blocks.head_at[-1])
        is_gate = (s >= first_gate) & (s <= blocks.gate_at[-1]) & no_head
        head = jnp.clip((s - LEAD + EVERY - 1) // EVERY, 0, H - 1)
        return jnp.where(is_gate, AT_GATE // BLOCK + gate(s), H - 1 - head)

    return blocks, pl.pallas_call(
        functools.partial(reduce_kernel, blocks=blocks),
        grid=(blocks.count + 10,),
        in_specs=[anywhere] * 6
        + [
            once((tokens, width)),
            across((tokens, BLOCK), down),
            pl.BlockSpec(
                (tokens, blocks.tail), lambda s: (0, blocks.downs * BLOCK // blocks.tail), pipeline_mode=pl.Buffered(1)
            ),
            pl.BlockSpec((2, tokens, BLOCK // 2), lambda s: (0, 0, up(s))),
            across((tokens, BLOCK), out),
            pl.BlockSpec((width, DV), lambda s: (0, AT_OUT // DV + starting(s))),
            across((tokens, DV), starting),
            across((tokens, DV), starting),
            once((1, DV)),
            across((tokens, DK), starting),
            across((width, BLOCK), win),
            pl.BlockSpec((width, LANES), lambda s: (0, AT_LOGIT // LANES), pipeline_mode=pl.Buffered(1)),
            once((8, width)),
            once((8, width)),
            across((rows, HC), coming),
            across((8, HC), coming),
            once((rows, LANES)),
            once((8, LANES)),
            once((tokens, LANES)),
            once((rows, LANES)),
            once(segr.shape),
            by_head((1, DK, DV)),
            once((2, H, DK, DK)),
            by_head((1, chunks, CHUNK, CHUNK)),
            by_head((1, tokens, DV + DK)),
            by_head((1, chunks, DK, DV)),
            by_head((1, chunks, DK, DK)),
            by_head((1, chunks, DK, DK)),
            by_head((1, chunks, CHUNK, DK)),
        ],
        out_specs=[anywhere, anywhere, whole((small, BLOCK))],
        out_shape=[
            jax.ShapeDtypeStruct((SPOTS * piece, blocks.count * BLOCK), BF16),
            jax.ShapeDtypeStruct((tokens, width), F32),
            jax.ShapeDtypeStruct((small, BLOCK), F32),
        ],
        scratch_shapes=[
            pltpu.VMEM((tokens, LANES), F32),
            pltpu.VMEM((8, HC), F32),
            pltpu.VMEM((8, LANES), F32),
            pltpu.VMEM((8, DV), F32),
            pltpu.VMEM((H, tokens, DV), BF16),
            pltpu.VMEM((H, tokens, DV), BF16),
            pltpu.VMEM((H, DK, DV), BF16),
            pltpu.VMEM((tokens, width), F32),
            pltpu.VMEM((2, tokens, width), BF16),
            pltpu.VMEM((4, small, BLOCK), F32),
            pltpu.VMEM((6, small, BLOCK), F32),
            pltpu.VMEM((tokens, LANES), F32),
            pltpu.VMEM((tokens, LANES), F32),
            pltpu.VMEM((tokens, LANES), F32),
            pltpu.VMEM((rows, HC), F32),
            pltpu.VMEM((tokens, HC), F32),
            pltpu.VMEM((rows + 8, HC), F32),
            pltpu.VMEM((4, width, tokens), BF16),
            pltpu.VMEM((rows, HC), BF16),
            pltpu.VMEM((H, HALO, HC), BF16),
            pltpu.VMEM((2, H, DK, DV), BF16),
            pltpu.VMEM((H, DK, DV), BF16),
            pltpu.VMEM((3, SPOTS, quarter, BLOCK), F32),
            pltpu.VMEM((3, SPOTS, quarter, BLOCK), BF16),
            pltpu.VMEM((4, SPOTS, quarter, BLOCK), BF16),
            pltpu.VMEM((4, 2, quarter, BLOCK), F32),
            pltpu.VMEM((4, 2, quarter, BLOCK), BF16),
            pltpu.VMEM((4, 2, quarter, BLOCK), BF16),
            pltpu.VMEM((4, PLANES, 2 * piece, BLOCK), F32),
            pltpu.VMEM((4, PLANES - 1, 2 * piece, BLOCK), BF16),
            pltpu.VMEM((4, PLANES - 1, 2 * piece, BLOCK), BF16),
            pltpu.VMEM((4, 2, 2 * piece, BLOCK), BF16),
            pltpu.VMEM((blocks.count, 2 * piece, BLOCK), BF16),
            pltpu.VMEM((4, 2, piece, BLOCK), BF16),
            pltpu.VMEM((4, 2, piece, BLOCK), BF16),
            pltpu.VMEM((4, 2, piece, BLOCK), BF16),
            sem((3,)), sem((4,)), sem((4,)), sem((4,)), sem((4,)), sem((4,)),
            sem((4, 2)), sem((blocks.count,)), sem((4,)), sem((4,)),
            sem((4, 2)), sem((blocks.count, 2)), sem((4, 2)),
            sem((H,)), sem((H,)), sem((2, H)), sem((2, H)),
            sem((4 + 2 * SPOTS,)), sem((6,)), sem((6,)),
        ],
        compiler_params=params(collective_id=1, has_side_effects=True),
        cost_estimate=cost(1e11, 1e8),
        name="reduce_gradients",
    )(
        d_out, hidden_mid, hidden, x, d_y, turn, d_mixer, act, act, d_gu, gated, weights, attn, gpre, gain_out, resp,
        weights, weights, gains, d_ffn, proj, taps, logits, par, cols, back, segr, state_in, maps, *saved,
    )


def unpack_kernel(
    sum_ref, query_ref, key_ref, value_ref, gate_ref, logit_ref, out_ref, wg_ref, wu_ref, wd_ref, *, blocks
):
    def part(n, low=0, high=BLOCK):
        return sum_ref[:, n * BLOCK + low : n * BLOCK + high].astype(F32)

    for h, n in enumerate(blocks.head_at):
        query_ref[:, h * DK : (h + 1) * DK] = part(n, 0, DK)
        key_ref[:, h * DK : (h + 1) * DK] = part(n, DK, 2 * DK)
        value_ref[:, h * DV : (h + 1) * DV] = part(n, 2 * DK, HC)
    for i, n in enumerate(blocks.gate_at):
        gate_ref[:, i * BLOCK : (i + 1) * BLOCK] = part(n)
    for i, n in enumerate(blocks.out_at):
        out_ref[i * BLOCK : (i + 1) * BLOCK, :] = jnp.transpose(part(n))
    middle = BLOCK // 2
    for i, n in enumerate(blocks.up_at):
        wg_ref[:, i * middle : (i + 1) * middle] = part(n, 0, middle)
        wu_ref[:, i * middle : (i + 1) * middle] = part(n, middle, BLOCK)
    for i, n in enumerate(blocks.down_at):
        wd_ref[i * BLOCK : (i + 1) * BLOCK, :] = jnp.transpose(part(n))
    last, tail = blocks.count - 1, blocks.tail
    wd_ref[blocks.downs * BLOCK :, :] = jnp.transpose(part(last, 0, tail))
    logit_ref[...] = part(last, tail, tail + LANES)


def unpack_gradients(blocks, sums):
    rows = sums.shape[0]
    inner = blocks.downs * BLOCK + blocks.tail
    shapes = [
        (rows, H * DK), (rows, H * DK), (rows, H * DV), (rows, H * DV), (rows, LANES), (H * DV, rows),
        (rows, inner), (rows, inner), (inner, rows),
    ]
    return pl.pallas_call(
        functools.partial(unpack_kernel, blocks=blocks),
        out_shape=[jax.ShapeDtypeStruct(shape, F32) for shape in shapes],
        compiler_params=params(),
        cost_estimate=cost(0, 6 * sums.size),
        name="unpack_gradients",
    )(sums)


def input_grad_kernel(
    dp_ref, dg_ref, dl_ref, w_ref, wl_ref, x_ref, gain_ref, dy_ref, out_ref, dgain_ref, acc_ref
):
    step = pl.program_id(0)

    @pl.when(step == 0)
    def _():
        acc_ref[...] = mm(dl_ref[...], wl_ref[...], NT)

    @pl.when(step < H)
    def _():
        acc_ref[...] += mm(dp_ref[...], w_ref[...], NT)

    @pl.when(step >= H)
    def _():
        acc_ref[...] += mm(dg_ref[...], w_ref[...], NT)

    @pl.when(step == pl.num_programs(0) - 1)
    def _():
        value = x_ref[...].astype(F32)
        size = lax.rsqrt(jnp.mean(value * value, axis=-1, keepdims=True) + 1e-06)
        unit = value * size
        d_hidden = acc_ref[...]
        dgain_ref[...] = jnp.zeros_like(dgain_ref)
        dgain_ref[0:1, :] = jnp.sum(d_hidden * unit, axis=0, keepdims=True)
        d_unit = d_hidden * gain_ref[...]
        out_ref[...] = dy_ref[...] + size * (
            d_unit - unit * jnp.mean(d_unit * unit, axis=-1, keepdims=True)
        )


def input_grad(d_proj, d_gpre, d_logit, weights, x, gain, d_y):
    tokens, width = x.shape
    block = HC
    second = d_gpre.shape[1] // block
    steps = H + second
    whole = lambda shape: pl.BlockSpec(shape, lambda j: (0,) * len(shape))
    late = lambda j: (0, jnp.maximum(j - H, 0))
    weight = lambda j: (0, jnp.where(j < H, H - 1 - j, j - H + AT_GATE // block))
    in_specs = [
        pl.BlockSpec((tokens, block), lambda j: (0, jnp.minimum(j, H - 1))),
        pl.BlockSpec((tokens, block), late),
        whole((tokens, LANES)),
        pl.BlockSpec((width, block), weight),
        pl.BlockSpec((width, LANES), lambda j: (0, AT_LOGIT // LANES)),
        whole((tokens, width)),
        whole((1, width)),
        whole((tokens, width)),
    ]
    return pl.pallas_call(
        input_grad_kernel,
        grid=(steps,),
        in_specs=in_specs,
        out_specs=[whole((tokens, width)), whole((8, width))],
        out_shape=[
            jax.ShapeDtypeStruct((tokens, width), F32),
            jax.ShapeDtypeStruct((8, width), F32),
        ],
        scratch_shapes=[pltpu.VMEM((tokens, width), F32)],
        compiler_params=params(),
        cost_estimate=cost(2 * tokens * width * steps * block, 3e7),
        name="input_grad",
    )(d_proj, d_gpre, d_logit, weights, weights, x, gain, d_y)


def shifted(block, axis, distance):
    devices = range(lax.axis_size(axis))
    route = [(i - distance, i) for i in devices if i - distance in devices]
    return lax.ppermute(block, axis, route)


def plain_sum(left, right, skip_left=0):
    part = lax.psum_scatter(outer(left, right, skip_left), "dp", scatter_dimension=0, tiled=True)
    return lax.psum(part, "seq").astype(F32)


def by_heads(query, key, value):
    lead = query.shape[:-1]
    parts = [query.reshape(lead + (H, DK)), key.reshape(lead + (H, DK)), value.reshape(lead + (H, DV))]
    return jnp.concatenate(parts, axis=-1).reshape(lead + (H * HC,))


def from_heads(value, heads=H):
    lead = value.shape[:-1]
    parts = value.reshape(lead + (heads, HC))
    return (
        parts[..., :DK].reshape(lead + (heads * DK,)),
        parts[..., DK : 2 * DK].reshape(lead + (heads * DK,)),
        parts[..., 2 * DK :].reshape(lead + (heads * DV,)),
    )


def token_rows(segments, place, tokens):
    ext = jnp.pad(segments, (HALO, LANES), constant_values=-1)
    ext = lax.dynamic_slice_in_dim(ext, place * tokens, tokens + LANES)
    seg = ext[HALO : HALO + tokens]
    blocks = seg.reshape(-1, CHUNK)
    before = ext[HALO - 1 : HALO - 1 + tokens : CHUNK]
    near = [seg] + [ext[HALO - j : HALO - j + tokens] == seg for j in range(1, CONV)]
    near += [(blocks == before[:, None]).reshape(-1), (blocks == blocks[:, -1:]).reshape(-1)]
    near = jnp.stack([row.astype(F32) for row in near])
    later = jnp.stack([(jnp.roll(ext, -j) == ext).astype(F32) for j in range(CONV)])
    return jnp.pad(near, ((0, 8 - near.shape[0]), (0, 0))), jnp.pad(later, ((0, 8 - CONV), (0, 0)))


def wide(value):
    return jnp.pad(value, ((0, 0), (0, LANES - value.shape[1])))


def local(
    inputs, segments, cotangent, norm_gain_mix, w_query, w_key, w_value, w_outgate, w_gates,
    conv_weight, decay_log, dt_bias, out_norm_gain, w_out, norm_gain_ffn, w_ffn_gate, w_ffn_up, w_ffn_down,
):
    tokens, width = inputs.shape[1:]
    place = lax.axis_index("seq")
    planned = (lax.axis_size("dp"), lax.axis_size("seq")) == (PLANES * CORES, SPOTS)
    low = lambda a: a.astype(BF16)
    inner = w_ffn_gate.shape[1]
    gain_out = out_norm_gain[None]
    taps_parts = by_heads(conv_weight[:, : H * DK], conv_weight[:, H * DK : 2 * H * DK], conv_weight[:, 2 * H * DK :])
    taps = jnp.pad(taps_parts, ((0, 8 - CONV), (0, 0)))
    par = jnp.pad(jnp.stack([decay_log, dt_bias]), ((0, 6), (0, LANES - H)))
    segr, later = token_rows(segments[0], place, tokens)

    if planned:
        gains = jnp.pad(jnp.stack([norm_gain_mix, norm_gain_ffn]), ((0, 6), (0, 0)))
        shards = (w_query, w_key, w_value, w_outgate, w_gates, w_out, w_ffn_gate, w_ffn_up, w_ffn_down)
        outs = mixer_forward(inputs[0], cotangent[0], shards, gains, gain_out, taps, par, segr, later)
        weights, hidden, x, d_out, turn, y1, hidden_mid, gains, cols, back, proj, logits, resp, *outs = outs
        saved, (maps, state_in, attn, gpre, gated) = outs[:6], outs[6:]
        gain_mix, gain_ffn = gains[0:1], gains[1:2]
    else:
        turn = jnp.eye(width, dtype=BF16)
        qkv = by_heads(low(w_query), low(w_key), low(w_value))
        qkv = jnp.concatenate([qkv[:, h * HC : (h + 1) * HC] for h in reversed(range(H))], axis=1)
        gates = jnp.pad(low(w_gates), ((0, 0), (0, AT_GATE - AT_LOGIT - 2 * H)))
        shard = [qkv, gates, low(w_outgate), low(w_out).T, low(w_ffn_gate), low(w_ffn_up), low(w_ffn_down).T]
        weights = lax.all_gather(jnp.concatenate(shard, axis=1), "dp", axis=0, tiled=True)
        gain_mix, gain_ffn = norm_gain_mix[None], norm_gain_ffn[None]
        cols = jnp.pad(segr.T, ((0, 0), (0, LANES - segr.shape[0])))
        back = jnp.pad(later.T[: tokens + HALO], ((0, 0), (0, LANES - later.shape[0])))
        x, d_out = inputs[0], cotangent[0]
        value = jnp.concatenate([shifted(x[tokens - HALO :], "seq", 1), x], axis=0).astype(F32)
        size = lax.rsqrt(jnp.mean(value * value, axis=-1, keepdims=True) + 1e-06)
        hidden = low(value * size * gain_mix)
        proj, logits, part, resp, exch, *saved = delta_forward(hidden, weights, taps, par, cols, segr)
        exch = lax.all_gather(exch[0], "seq")
        slots = jnp.arange(exch.shape[0], dtype=jnp.int32)
        place_arr = place.reshape((1,)).astype(jnp.int32)
        gpre = outgate(hidden, weights)
        state_in, attn, gated, y1, hidden_mid = mixer_out(
            place_arr, slots, part, resp, exch, gpre, gain_out, weights, x, gain_ffn
        )
    result, act, d_gu, d_y, d_mixer, d_gain_ffn = feed_forward(
        hidden_mid, d_out, y1, gain_ffn, turn, weights, inner
    )
    if planned:
        blocks, (sums, d_inputs, small) = reduce_gradients(
            d_out, hidden_mid, hidden, x, d_y, turn, d_mixer, act, d_gu, gated, weights, attn, gpre, gain_out, resp,
            gains, d_gain_ffn, proj, taps, logits, par, cols, back, segr, state_in, maps, saved,
        )
        g_query, g_key, g_value, g_og, g_gates, g_out, g_gate, g_up, g_down = unpack_gradients(blocks, sums)
        d_taps = small[: 8 * H].reshape(H, 8, HC)[:, :CONV].transpose(1, 0, 2).reshape(CONV, H * HC)
        rest = small[8 * H :]
        d_gains = jnp.concatenate([rest[:2], rest[8:10]], axis=1)
        d_gain_mix, d_gain_ffn = d_gains[0], d_gains[1]
        d_gain_out, d_par = rest[16, :DV], rest[16:18, DV : DV + H]
        d_conv = jnp.concatenate(from_heads(d_taps), axis=1)
        d_decay_log, d_dt_bias = d_par[0], d_par[1]
    else:
        d_attn, d_gpre, local_grad, d_gain_out = mixer_back(d_mixer, weights, attn, gpre, gain_out, resp)
        grads = lax.all_gather(local_grad, "seq")
        d_proj, d_logits, d_taps, d_par = delta_backward(
            place_arr, slots, proj, taps, logits, par, cols, back, segr, d_attn, state_in, exch, grads, saved
        )
        sent_back = shifted(d_proj[:HALO], "seq", -1)
        d_proj = d_proj.at[tokens:].add(sent_back)[HALO:]
        d_logit = low(d_logits)
        g_down = plain_sum(d_out, act).T
        g_gate = plain_sum(hidden_mid, d_gu[0])
        g_up = plain_sum(hidden_mid, d_gu[1])
        g_out = plain_sum(d_mixer, gated).T
        g_og = plain_sum(hidden, d_gpre, HALO)
        g_query, g_key, g_value = from_heads(plain_sum(hidden, d_proj, HALO))
        g_gates = plain_sum(hidden, d_logit, HALO)
        d_inputs, d_gain_mix = input_grad(d_proj, d_gpre, d_logit, weights, x, gain_mix, d_y)
        d_conv = jnp.concatenate(from_heads(d_taps[:CONV]), axis=1)
        d_gain_mix, d_conv, d_decay_log, d_dt_bias, d_gain_out, d_gain_ffn = lax.psum(
            (d_gain_mix[0], d_conv, d_par[0, :H], d_par[1, :H], d_gain_out[0], d_gain_ffn[0]), ("dp", "seq")
        )
    return (
        result[None], d_inputs[None], d_gain_mix, g_query, g_key, g_value, g_og,
        g_gates[:, : 2 * H], d_conv, d_decay_log, d_dt_bias, d_gain_out, g_out,
        d_gain_ffn, g_gate, g_up, g_down,
    )


def solution(mesh):
    rows, cols, copied = P("dp", None), P(None, "dp"), P()
    tokens = P("dp", "seq", None)
    in_specs = (
        tokens, rows, tokens, copied, rows, rows, rows, rows, rows,
        copied, copied, copied, copied, cols, copied, rows, rows, cols,
    )
    out_specs = (
        tokens, tokens, copied, rows, rows, rows, rows, rows,
        copied, copied, copied, copied, cols, copied, rows, rows, cols,
    )
    return jax.shard_map(local, mesh=mesh, in_specs=in_specs, out_specs=out_specs, check_vma=False)
```

profile of v0, /device:TPU:8, one launch (start us, length us, event | category | flops | bytes accessed | tf_op | source)
XLA Modules:
  0.0 458.9 jit_solution(18341789887951692602)
XLA Ops:
  0.7 1.4 copy.45.wl_in
  2.1 1.3 select_maximum_fusion.gains_ref
  3.4 0.8 slice.103
  4.2 0.7 slice_bitcast_fusion.5
  5.0 0.7 pad.25.taps_ref
  5.7 1.3 select_maximum_fusion.1.par_ref
  6.9 0.8 pad_dynamic-slice_fusion
  7.7 0.1 slice_bitcast_fusion.6
  7.8 0.2 slice_reduce_fusion
  8.0 0.1 slice.108
  8.1 0.1 fusion.8
  8.2 0.6 pad.28.near_ref.segr_ref
  8.8 0.5 slice.111
  9.3 0.1 slice.110
  9.4 0.1 slice.114
  9.4 0.1 slice.112
  9.5 1.4 fusion.3
  11.0 0.1 pad_maximum_fusion.1
  11.1 0.6 pad.29.later_ref
  11.7 163.0 %mixer_forward.1 = (bf16[1024,17152]{1,0:T(8,128)(2,1)}, bf16[528,1024]{1,0:T(8,128)(2,1)}, bf16[512,1024]{1,0:T(8,128)(2,1)}, bf16[512,1024]{1,0:T(8,128)(2,1)}...) custom-call(bf16[512,1024]{1,0:T(8,128)(2,1)} %bitcast.80, ...), custom_call_target="tpu_custom_call" | custom-call | flops 99999997952 | bytes 100000000 | tf_op jit(solution)/shard_map/mixer_forward/pallas_call | solution.py:775
  174.7 1.4 slice.116.gain_ref
  176.0 29.7 %feed_forward.1 = (bf16[512,1024]{1,0:T(8,128)(2,1)}, bf16[512,2816]{1,0:T(8,128)(2,1)}, bf16[2,512,2816]{2,1,0:T(8,128)(2,1)}, f32[512,1024]{1,0:T(8,128)}, bf1...) custom-call(bf16[512,1024]{1,0:T(8,128)(2,1)} %get-tuple-element.59.h_ref.hmid_any, ...), custom_call_target="tpu_custom_call" | custom-call | flops 17716740096 | bytes 30000000 | tf_op jit(solution)/shard_map/feed_forward/pallas_call | solution.py:1266
  205.8 239.3 %reduce_gradients.1 = (bf16[128,16896]{1,0:T(8,128)(2,1)}, f32[512,1024]{1,0:T(8,128)}, f32[88,512]{1,0:T(8,128)}) custom-call(bf16[512,1024]{1,0:T(8,128)(2,1)} %get-tuple-element.60.dout_ref.dout_any, bf16[512,1024]{1,0:T(8,128)(2,1)} %get-tuple-element.59.h_ref.hmid_any, bf16[528,1024]{1,0:T(8,128)(2,1)} %get-tuple-element.66.hidden_any, ...), custom_call_target="tpu_custom_call" | custom-call | flops 99999997952 | bytes 100000000 | tf_op jit(solution)/shard_map/reduce_gradients/pallas_call | solution.py:1846
  445.1 0.7 fusion.9
  445.8 0.6 pad_maximum_fusion.2
  446.4 0.0 copy-start
  446.4 5.8 %unpack_gradients.1 = (f32[128,1024]{1,0:T(8,128)}, f32[128,1024]{1,0:T(8,128)}, f32[128,2048]{1,0:T(8,128)}, f32[128,2048]{1,0:T(8,128)}, f32[128,128]{1,0:T(8,...) custom-call(bf16[128,16896]{1,0:T(8,128)(2,1)} %get-tuple-element.91.sum_ref), custom_call_target="tpu_custom_call" | custom-call | bytes 12976128 | tf_op jit(solution)/shard_map/unpack_gradients/pallas_call | solution.py:1973
  452.3 1.5 copy.49
  453.8 0.0 copy-done
  453.8 0.6 pad_maximum_fusion
  454.5 0.5 slice_bitcast_fusion.7
  455.0 0.6 slice.128
  455.6 3.2 copy.59
  (15 shorter events, 0.2 us)
Async XLA Ops:
  446.4 7.4 %copy-start = (f32[88,512]{1,0:T(8,128)S(1)}, f32[88,512]{1,0:T(8,128)}, u32[]{:S(2)}) copy-start(f32[88,512]{1,0:T(8,128)} %get-tuple-element.90) | copy-start | bytes 540676
where the time goes:
time: 465 us; the launch traced here: 459 us
  Pallas kernels  438 us (94%)
  local copies, waits for them, and re-layouts  14.6 us (3%)
  other arithmetic  5.51 us (1%)
    pallas_call x1, Pallas kernels, reduce_gradients(): pl.pallas_call(functools.partial(reduce_kernel, blocks=blocks), grid=(blo...  239 us
    pallas_call x1, Pallas kernels, mixer_forward(): pl.pallas_call(functools.partial(mixer_forward_kernel, spans=spans, inner...  163 us
    pallas_call x1, Pallas kernels, feed_forward(): pl.pallas_call(ffn_kernel, grid=(inner // block,), in_specs=[whole((token...  29.7 us

commit v1 on v0

--- a/solution.py
+++ b/solution.py
@@ -143,6 +143,20 @@
     for c in range(logits.shape[0] // CHUNK):
         part = decay_ref[c * CHUNK : (c + 1) * CHUNK, :]
         cum_ref[c * CHUNK : (c + 1) * CHUNK, :] = mm_exact(lower, part)
+
+
+def join_taps(taps_ref, query_ref, key_ref, value_ref):
+    taps_ref[0:CONV, :DK] = query_ref[...]
+    taps_ref[0:CONV, DK : 2 * DK] = key_ref[...]
+    taps_ref[0:CONV, 2 * DK :] = value_ref[...]
+
+
+def taps_specs(at):
+    return [
+        pl.BlockSpec((CONV, DK), lambda s: (0, at(s))),
+        pl.BlockSpec((CONV, DK), lambda s: (0, H + at(s))),
+        pl.BlockSpec((CONV, DV), lambda s: (0, 2 * H * DK // DV + at(s))),
+    ]
 
 
 def mix_taps(p_ref, taps_ref, cols, pf_ref):
@@ -497,18 +511,25 @@
 
 
 def mixer_forward_kernel(
-    x_ref, cot_ref, wq_ref, wk_ref, wv_ref, wo_ref, wl_in, wm_ref, wg_ref, wu_ref, wd_ref,
-    gains_ref, gain_ref, taps_ref, par_ref, near_ref, later_ref,
+    x_ref, wq_ref, wk_ref, wv_ref, wl_in, gain_mix_ref, gain_ffn_ref, gain_ref, rate_ref, bias_ref, seg_ref,
+    taps_q_ref, taps_k_ref, taps_v_ref, cot_any, wo_any, wm_any, wg_any, wu_any, wd_any,
     full_ref, hidden_out, x_out, cot_out, turn_out, y_out, mid_out,
-    gains_out, cols_ref, back_ref, p_ref, logit_ref, resp_out,
+    gains_out, near_ref, par_ref, cols_ref, back_ref, p_ref, logit_ref, resp_out,
     inv_ref, upd_ref, st_ref, stm_ref, amap_ref, rmap_ref, maps_ref, sin_ref, attn_ref, gpre_ref, gated_ref,
     shard_ref, hidden_ref, xs_ref, cots_ref, turn_ref, y_ref, mid_ref, xh_ref, part_ref, resp_ref, exch_ref, stage_ref, half_ref, low_ref,
     beta_ref, decay_ref, cum_ref, pf_ref, mix_ref, w_ref, wl_ref, wb_ref,
+    cot_ref, wo_ref, wm_ref, wg_ref, wu_ref, wd_ref, taps_ref, row_ref, later_ref, late_sem,
     send_sem, recv_sem, local_sem, exch_send, exch_recv, load_sem, pair_sem, out_sem, halo_sem, *, spans, inner,
 ):
     step = pl.program_id(0)
     place = lax.axis_index("seq")
     tokens, width = x_ref.shape
+
+    def late(which):
+        source, to = (
+            (wo_any, wo_ref), (wm_any, wm_ref), (wg_any, wg_ref), (wu_any, wu_ref), (wd_any, wd_ref), (cot_any, cot_ref),
+        )[which]
+        return pltpu.make_async_copy(source, to, late_sem.at[which])
 
     def pack(at, size):
         while size > 0:
@@ -519,16 +540,23 @@
                 shard_ref[:, at + 2 * DK : at + HC] = wv_ref[:, head * DV : (head + 1) * DV].astype(BF16)
             elif at < AT_GATE:
                 span = LANES
-                shard_ref[:, at : at + LANES] = jnp.zeros((shard_ref.shape[0], LANES), BF16)
-                shard_ref[:, at : at + 2 * H] = wl_in[...].astype(BF16)
+                rest = jnp.zeros((LANES - 2 * H, LANES), F32)
+                turned = jnp.transpose(jnp.concatenate([wl_in[...], rest], axis=0))
+                shard_ref[:, at : at + LANES] = turned.astype(BF16)
             elif at < AT_OUT:
                 span, low = size, at - AT_GATE
+                if low == 0:
+                    late(0).wait()
                 shard_ref[:, at : at + span] = wo_ref[:, low : low + span].astype(BF16)
             elif at < AT_FFN:
                 span, low = size, at - AT_OUT
+                if low == 0:
+                    late(1).wait()
                 shard_ref[:, at : at + span] = jnp.transpose(wm_ref[low : low + span, :]).astype(BF16)
             else:
                 span, which, low = size, (at - AT_FFN) // inner, (at - AT_FFN) % inner
+                if low == 0:
+                    late(2 + which).wait()
                 if which < 2:
                     shard_ref[:, at : at + span] = (wg_ref, wu_ref)[which][:, low : low + span].astype(BF16)
                 else:
@@ -608,6 +636,8 @@
             give_halo().start()
 
         gathering.tick(0)
+        for which in range(6):
+            late(which).start()
         at = iota2((1, width), 1)
         piece = width // (PLANES * CORES * SPOTS)
         core, rest = at // (width // 2), at % (width // 2)
@@ -619,21 +649,42 @@
         turn_ref[...] = jnp.where(iota2((width, width), 0) == order, 1.0, 0.0).astype(BF16)
         keep(3).start()
         gathering.tick(1)
-        cots_ref[...] = mm(cot_ref[...], turn_ref[...]).astype(BF16)
-        keep(2).start()
-        high, mid = halves(gains_ref[...])
-        rest = (gains_ref[...] - high.astype(F32)) - mid.astype(F32)
+        gains = jnp.concatenate([gain_mix_ref[...], gain_ffn_ref[...], jnp.zeros((6, width), F32)], axis=0)
+        high, mid = halves(gains)
+        rest = (gains - high.astype(F32)) - mid.astype(F32)
         gains_out[...] = mm(high, turn_ref[...]) + mm(mid, turn_ref[...]) + mm(rest, turn_ref[...])
+        par_ref[...] = jnp.zeros_like(par_ref)
+        par_ref[0:1, :H] = rate_ref[...]
+        par_ref[1:2, :H] = bias_ref[...]
         gathering.tick(2)
-        blank = jnp.zeros((LANES - near_ref.shape[0], LANES), F32)
+
+        row_ref[...] = jnp.full(row_ref.shape, -1.0, F32)
+        row_ref[0:1, LANES : LANES + seg_ref.shape[1]] = seg_ref[...].astype(F32)
+        row = row_ref[0:1, pl.ds(pl.multiple_of(place * tokens, LANES), tokens + 2 * LANES)]
+        seg = row[:, LANES : LANES + tokens]
+        near = [seg]
+        for j in range(1, CONV):
+            moved = pltpu.roll(row, j, 1)[:, LANES : LANES + tokens]
+            near.append((moved == seg).astype(F32))
+        before, last = [], []
+        for n in range(tokens // CHUNK):
+            part = seg[:, n * CHUNK : (n + 1) * CHUNK]
+            before.append((part == row[:, LANES + n * CHUNK - 1 : LANES + n * CHUNK]).astype(F32))
+            last.append((part == part[:, CHUNK - 1 :]).astype(F32))
+        near += [jnp.concatenate(before, axis=1), jnp.concatenate(last, axis=1)]
+        near.append(jnp.zeros((8 - len(near), tokens), F32))
+        near_ref[...] = jnp.concatenate(near, axis=0)
+        size = row.shape[1]
+        ahead = pltpu.roll(row, size - (LANES - HALO), 1)
+        later = [jnp.zeros((1, tokens + LANES), F32)]
+        for j in range(1, CONV):
+            later.append((pltpu.roll(ahead, size - j, 1) == ahead).astype(F32)[:, : tokens + LANES])
+        later.append(jnp.zeros((8 - CONV, tokens + LANES), F32))
+        later_ref[...] = jnp.concatenate(later, axis=0)
+        blank = jnp.zeros((LANES - 8, LANES), F32)
         for n in range(tokens // LANES):
             span = slice(n * LANES, (n + 1) * LANES)
             cols_ref[span, :] = jnp.transpose(jnp.concatenate([near_ref[:, span], blank], axis=0))
-        for n in range(tokens // LANES + 1):
-            span = slice(n * LANES, (n + 1) * LANES)
-            turned = jnp.transpose(jnp.concatenate([later_ref[:, span], blank], axis=0))
-            kept = min(LANES, tokens + HALO - n * LANES)
-            back_ref[n * LANES : n * LANES + kept, :] = turned[:kept]
         gathering.tick(3)
 
         @pl.when(place > 0)
@@ -677,6 +728,7 @@
                 def _(h=h):
                     gathering.tick(lead + 2 * h)
 
+        join_taps(taps_ref, taps_q_ref, taps_k_ref, taps_v_ref)
         state = forward_head(
             head, p_ref, taps_ref, cols_ref, near_ref, part_ref.at[head], resp_ref.at[head], inv_ref, upd_ref,
             st_ref, stm_ref, amap_ref, rmap_ref, beta_ref, cum_ref, pf_ref, mix_ref, between,
@@ -733,6 +785,15 @@
         @pl.when(head == 0)
         def _():
             y_ref[...] = xs_ref[...].astype(F32)
+            late(5).wait()
+            cots_ref[...] = mm(cot_ref[...], turn_ref[...]).astype(BF16)
+            keep(2).start()
+            blank = jnp.zeros((LANES - 8, LANES), F32)
+            for n in range(tokens // LANES + 1):
+                span = slice(n * LANES, (n + 1) * LANES)
+                turned = jnp.transpose(jnp.concatenate([later_ref[:, span], blank], axis=0))
+                kept = min(LANES, tokens + HALO - n * LANES)
+                back_ref[n * LANES : n * LANES + kept, :] = turned[:kept]
 
         y_ref[...] += mm(gated, wb_ref[slot, 1], NT)
 
@@ -753,11 +814,12 @@
                 keep(which).wait()
 
 
-def mixer_forward(x, cotangent, shards, gains, gain, taps, par, near, later):
+def mixer_forward(x, cotangent, shards, gains, gain, rate, bias, segments, taps):
     tokens, width = x.shape
     rows = tokens + HALO
     chunks = tokens // CHUNK
-    inner = shards[-1].shape[0]
+    query, key, value, outgate_w, gates, out_w, gate_w, up_w, down_w = shards
+    inner = down_w.shape[0]
     spans = gather_spans(inner)
     total = AT_FFN + 3 * inner
     once = lambda array: pl.BlockSpec(
@@ -775,12 +837,14 @@
     return pl.pallas_call(
         functools.partial(mixer_forward_kernel, spans=spans, inner=inner),
         grid=(2 * H,),
-        in_specs=[once(a) for a in (x, cotangent, *shards, gains, gain)]
-        + [across((8, HC), early)]
-        + [once(a) for a in (par, near, later)],
+        in_specs=[once(a) for a in (x, query, key, value, gates, *gains, gain, rate, bias, segments)]
+        + taps_specs(early)
+        + [anywhere] * 6,
         out_specs=[anywhere] * 7
         + [
             whole((8, width)),
+            whole((8, tokens)),
+            whole((8, LANES)),
             whole((tokens, LANES)),
             whole((rows, LANES)),
             across((rows, HC), early),
@@ -804,6 +868,8 @@
             shape((tokens, width), F32),
             shape((tokens, width), BF16),
             shape((8, width), F32),
+            shape((8, tokens), F32),
+            shape((8, LANES), F32),
             shape((tokens, LANES), F32),
             shape((rows, LANES), F32),
             shape((rows, H * HC), BF16),
@@ -819,7 +885,7 @@
             shape((tokens, H * DV), BF16),
         ],
         scratch_shapes=[
-            pltpu.VMEM((shards[0].shape[0], total), BF16),
+            pltpu.VMEM((query.shape[0], total), BF16),
             pltpu.VMEM((rows, width), BF16),
             pltpu.VMEM((tokens, width), BF16),
             pltpu.VMEM((tokens, width), BF16),
@@ -841,6 +907,16 @@
             pltpu.VMEM((width, HC), BF16),
             pltpu.VMEM((width, LANES), BF16),
             pltpu.VMEM((2, 2, width, DV), BF16),
+            pltpu.VMEM(cotangent.shape, BF16),
+            pltpu.VMEM(outgate_w.shape, F32),
+            pltpu.VMEM(out_w.shape, F32),
+            pltpu.VMEM(gate_w.shape, F32),
+            pltpu.VMEM(up_w.shape, F32),
+            pltpu.VMEM(down_w.shape, F32),
+            pltpu.VMEM((8, HC), F32),
+            pltpu.VMEM((8, segments.shape[1] + 2 * LANES), F32),
+            pltpu.VMEM((8, tokens + LANES), F32),
+            sem((6,)),
             sem((len(spans), 10)),
             sem((len(spans), 7)),
             sem((len(spans), SPOTS)),
@@ -854,7 +930,10 @@
         compiler_params=params(collective_id=0, has_side_effects=True),
         cost_estimate=cost(1e11, 1e8),
         name="mixer_forward",
-    )(x, cotangent, *shards, gains, gain, taps, par, near, later)
+    )(
+        x, query, key, value, gates, *gains, gain, rate, bias, segments, taps, taps, taps,
+        cotangent, outgate_w, out_w, gate_w, up_w, down_w,
+    )
 
 
 def backward_kernel(place_ref, slot_ref, *refs):
@@ -872,39 +951,60 @@
     d_state = lax.fori_loop(
         0, places - 1, lambda lap, grad: behind(places - 1 - lap, grad), jnp.zeros((DK, DV), F32)
     )
-    backward_head(pl.program_id(0), d_state, *refs)
+    for phase in range(PHASES):
+        backward_head(phase, pl.program_id(0), lambda: d_state, *refs)
+
+
+PHASES = 3
 
 
 def backward_head(
-    head, d_state, p_ref, taps_ref, logit_ref, par_ref, cols_ref, back_ref, segr_ref,
+    phase, head, entering, p_ref, taps_ref, logit_ref, par_ref, cols_ref, back_ref, segr_ref,
     dattn_ref, sin_ref,
     inv_ref, upd_ref, st_ref, stm_ref, amap_ref, rmap_ref,
     dp_ref, dlogit_ref, dtaps_ref, dpar_ref,
-    beta_ref, decay_ref, cum_ref, pf_ref, pre_ref, dmix_ref,
+    beta_ref, decay_ref, cum_ref, pf_ref, pre_ref, dmix_ref, dstate_ref, dbeta_ref, ddecay_ref,
 ):
-    @pl.when(head == 0)
-    def _():
-        gate_tables(logit_ref, par_ref, beta_ref, decay_ref, cum_ref)
-        dlogit_ref[...] = jnp.zeros_like(dlogit_ref)
-        dpar_ref[...] = jnp.zeros_like(dpar_ref)
-
+    tokens = cols_ref.shape[0]
+    chunks = range(tokens // CHUNK)
+    refs = (
+        cols_ref, segr_ref, dattn_ref, sin_ref, inv_ref, upd_ref, st_ref, stm_ref, beta_ref, cum_ref, pre_ref,
+        dmix_ref, dstate_ref, dbeta_ref, ddecay_ref,
+    )
+    if phase == 0:
+
+        @pl.when(head == 0)
+        def _():
+            gate_tables(logit_ref, par_ref, beta_ref, decay_ref, cum_ref)
+            dlogit_ref[...] = jnp.zeros_like(dlogit_ref)
+            dpar_ref[...] = jnp.zeros_like(dpar_ref)
+
+        pre_ref[...] = mix_taps(p_ref, taps_ref, cols_ref[...], pf_ref)
+        d_state = entering()
+        for c in reversed(chunks):
+            rows = slice(c * CHUNK, (c + 1) * CHUNK)
+            dstate_ref[c] = d_state
+            if c > 0:
+                d_state = mm(amap_ref[0, c], d_state, TN) + mm(rmap_ref[0, c], dattn_ref[rows, :], TN)
+        backward_chunks(head, chunks[:1], *refs)
+    elif phase == 1:
+        backward_chunks(head, chunks[1:3], *refs)
+    else:
+        backward_chunks(head, chunks[3:], *refs)
+        backward_ends(
+            head, taps_ref, logit_ref, par_ref, cols_ref, back_ref, dp_ref, dlogit_ref, dtaps_ref, dpar_ref,
+            beta_ref, decay_ref, pf_ref, dmix_ref, dbeta_ref, ddecay_ref,
+        )
+
+
+def backward_chunks(
+    head, chunks, cols_ref, segr_ref, dattn_ref, sin_ref, inv_ref, upd_ref, st_ref, stm_ref, beta_ref, cum_ref, pre_ref,
+    dmix_ref, dstate_ref, dbeta_ref, ddecay_ref,
+):
     cols = cols_ref[...]
-    tokens = cols.shape[0]
-    chunks = range(tokens // CHUNK)
-    pre = mix_taps(p_ref, taps_ref, cols, pf_ref)
-    pre_ref[...] = pre
     beta = lane(beta_ref[...], head + H)
-
     state_in = sin_ref[0]
-    d_states = [None] * len(chunks)
-    for c in reversed(chunks):
-        rows = slice(c * CHUNK, (c + 1) * CHUNK)
-        d_states[c] = d_state
-        if c > 0:
-            d_state = mm(amap_ref[0, c], d_state, TN) + mm(rmap_ref[0, c], dattn_ref[rows, :], TN)
-
     row_ids, col_ids = iota2((CHUNK, CHUNK), 0), iota2((CHUNK, CHUNK), 1)
-    d_beta_all, d_decay_all = [], []
     for c in chunks:
         rows = slice(c * CHUNK, (c + 1) * CHUNK)
         mixed = pre_ref[rows, :]
@@ -928,7 +1028,7 @@
             state = st_ref[0, c] + mm(stm_ref[0, c], state_in)
         updates = upd_ref[0, rows, :DV] - mm(upd_ref[0, rows, DV:], state)
         d_attn = dattn_ref[rows, :]
-        d_state = d_states[c]
+        d_state = dstate_ref[c]
         d_updates = mm(scores, d_attn, TN) + mm(last * key, d_state)
         solved = mm(inv_ref[0, c], d_updates, TN)
         both = jnp.concatenate([d_attn, solved.astype(BF16)], axis=0)
@@ -973,8 +1073,8 @@
         d_decay = jnp.sum(
             jnp.where(row_ids <= col_ids, to_row(d_cum), 0.0), axis=1, keepdims=True
         )
-        d_beta_all.append(d_beta)
-        d_decay_all.append(d_decay)
+        dbeta_ref[rows, :] = jnp.broadcast_to(d_beta, (CHUNK, LANES))
+        ddecay_ref[rows, :] = jnp.broadcast_to(d_decay, (CHUNK, LANES))
         d_query = d_query * DK**-0.5
         d_query = query_size * (
             d_query - query_unit * jnp.sum(d_query * query_unit, axis=1, keepdims=True)
@@ -985,14 +1085,19 @@
             [d_query, d_key, d_value], axis=1
         )
 
-    d_beta = jnp.concatenate(d_beta_all, axis=0)
-    d_decay = jnp.concatenate(d_decay_all, axis=0)
+
+def backward_ends(
+    head, taps_ref, logit_ref, par_ref, cols_ref, back_ref, dp_ref, dlogit_ref, dtaps_ref, dpar_ref,
+    beta_ref, decay_ref, pf_ref, dmix_ref, dbeta_ref, ddecay_ref,
+):
+    cols = cols_ref[...]
+    tokens = cols.shape[0]
     lanes = iota2((tokens, LANES), 1)
     slope = jax.nn.sigmoid(logit_ref[HALO:, :] + par_ref[1:2, :]) * -jnp.exp(par_ref[0:1, :])
-    here = jnp.where(lanes == head, d_decay, 0.0)
+    here = jnp.where(lanes == head, ddecay_ref[...], 0.0)
     d_first = here * slope
     strengths = beta_ref[...]
-    d_second = jnp.where(lanes == head + H, d_beta, 0.0) * strengths * (1.0 - strengths)
+    d_second = jnp.where(lanes == head + H, dbeta_ref[...], 0.0) * strengths * (1.0 - strengths)
     dlogit_ref[...] += d_first + d_second
     dpar_ref[0:1, :] += jnp.sum(here * decay_ref[...], axis=0, keepdims=True)
     dpar_ref[1:2, :] += jnp.sum(d_first, axis=0, keepdims=True)
@@ -1065,6 +1170,9 @@
             pltpu.VMEM((rows, HC), F32),
             pltpu.VMEM((tokens, HC), F32),
             pltpu.VMEM((rows + 8, HC), F32),
+            pltpu.VMEM((chunks, DK, DV), F32),
+            pltpu.VMEM((tokens, LANES), F32),
+            pltpu.VMEM((tokens, LANES), F32),
         ],
         compiler_params=params(),
         cost_estimate=cost(8e9 * H, 5e6 * H),
@@ -1214,31 +1322,54 @@
 
 
 def ffn_kernel(
-    h_ref, dout_ref, y_ref, gain_ref, turn_ref, wg_ref, wu_ref, wd_ref,
-    out_ref, act_ref, dgu_ref, dy_ref, dmix_ref, dgain_ref, res_ref, dh_ref,
+    h_ref, dout_ref, y_ref, gain_ref, turn_ref, weights_ref,
+    out_ref, act_ref, dgu_ref, dy_ref, dmix_ref, dgain_ref,
+    w_ref, acts_ref, dg_ref, du_ref, res_ref, dh_ref, load_sem, *, inner, block, gain_row,
 ):
     step = pl.program_id(0)
+    blocks = inner // block
+    across = dh_ref.shape[1] // (pl.num_programs(0) - blocks)
+
+    def load(which, n):
+        cols = pl.multiple_of(n * block, block)
+        return pltpu.make_async_copy(
+            weights_ref.at[:, pl.ds(AT_FFN + which * inner + cols, block)],
+            w_ref.at[which, :, pl.ds(cols, block)],
+            load_sem.at[which, n],
+        )
 
     @pl.when(step == 0)
     def _():
-        res_ref[...] = y_ref[...]
-        dh_ref[...] = jnp.zeros_like(dh_ref)
-
-    hidden = h_ref[...]
-    w_gate, w_up, w_down = wg_ref[...], wu_ref[...], wd_ref[...]
-    gate = mm(hidden, w_gate)
-    up = mm(hidden, w_up)
-    d_act = mm(dout_ref[...], w_down)
-    slope = jax.nn.sigmoid(gate)
-    swish = gate * slope
-    act = (swish * up).astype(BF16)
-    act_ref[...] = act
-    d_gate = (d_act * up * slope * (1.0 + gate * (1.0 - slope))).astype(BF16)
-    d_up = (d_act * swish).astype(BF16)
-    dgu_ref[0] = d_gate
-    dgu_ref[1] = d_up
-    res_ref[...] += mm(act, w_down, NT)
-    dh_ref[...] += mm(d_gate, w_gate, NT) + mm(d_up, w_up, NT)
+        for n in range(blocks):
+            for which in range(3):
+                load(which, n).start()
+
+    @pl.when(step < blocks)
+    def _():
+        for which in range(3):
+            load(which, step).wait()
+        cols = pl.ds(pl.multiple_of(step * block, block), block)
+        hidden = h_ref[...]
+        gate = mm(hidden, w_ref[0, :, cols])
+        up = mm(hidden, w_ref[1, :, cols])
+        d_act = mm(dout_ref[...], w_ref[2, :, cols])
+        slope = jax.nn.sigmoid(gate)
+        swish = gate * slope
+        act = (swish * up).astype(BF16)
+        act_ref[...] = act
+        acts_ref[:, cols] = act
+        d_gate = (d_act * up * slope * (1.0 + gate * (1.0 - slope))).astype(BF16)
+        d_up = (d_act * swish).astype(BF16)
+        dgu_ref[0] = d_gate
+        dg_ref[:, cols] = d_gate
+        dgu_ref[1] = d_up
+        du_ref[:, cols] = d_up
+
+    @pl.when(step >= blocks)
+    def _():
+        rows = pl.ds(pl.multiple_of((step - blocks) * across, across), across)
+        res_ref[:, rows] = y_ref[:, rows] + mm(acts_ref[...], w_ref[2, rows, :], NT)
+        dh_ref[:, rows] = mm(dg_ref[...], w_ref[0, rows, :], NT) + mm(du_ref[...], w_ref[1, rows, :], NT)
 
     @pl.when(step == pl.num_programs(0) - 1)
     def _():
@@ -1249,7 +1380,7 @@
         d_hidden = dh_ref[...]
         dgain_ref[...] = jnp.zeros_like(dgain_ref)
         dgain_ref[0:1, :] = jnp.sum(d_hidden * unit, axis=0, keepdims=True)
-        d_unit = d_hidden * gain_ref[...]
+        d_unit = d_hidden * gain_ref[gain_row : gain_row + 1, :]
         d_y = dout_ref[...].astype(F32) + size * (
             d_unit - unit * jnp.mean(d_unit * unit, axis=-1, keepdims=True)
         )
@@ -1257,25 +1388,28 @@
         dmix_ref[...] = d_y.astype(BF16)
 
 
-def feed_forward(hidden, d_out, y1, gain, turn, weights, inner):
+def feed_forward(hidden, d_out, y1, gains, gain_row, turn, weights, inner):
     tokens, width = hidden.shape
-    block = 256
-    weight = lambda at: pl.BlockSpec((width, block), lambda j: (0, j + at // block))
+    block, across = 256, 256
+    blocks = inner // block
+    once = lambda shape: pl.BlockSpec(shape, lambda j: (0,) * len(shape), pipeline_mode=pl.Buffered(1))
     whole = lambda shape: pl.BlockSpec(shape, lambda j: (0,) * len(shape))
-    across = pl.BlockSpec((tokens, block), lambda j: (0, j))
+    at = lambda j: jnp.minimum(j, blocks - 1)
     return pl.pallas_call(
-        ffn_kernel,
-        grid=(inner // block,),
+        functools.partial(ffn_kernel, inner=inner, block=block, gain_row=gain_row),
+        grid=(blocks + width // across,),
         in_specs=[
+            once((tokens, width)),
+            once((tokens, width)),
+            once((tokens, width)),
+            once(gains.shape),
+            once((width, width)),
+            pl.BlockSpec(memory_space=pl.ANY),
+        ],
+        out_specs=[
             whole((tokens, width)),
-            whole((tokens, width)),
-            whole((tokens, width)),
-            whole((1, width)),
-            pl.BlockSpec((width, width), lambda j: (0, 0), pipeline_mode=pl.Buffered(1)),
-        ]
-        + [weight(AT_FFN + i * inner) for i in range(3)],
-        out_specs=[
-            whole((tokens, width)), across, pl.BlockSpec((2, tokens, block), lambda j: (0, 0, j)),
+            pl.BlockSpec((tokens, block), lambda j: (0, at(j))),
+            pl.BlockSpec((2, tokens, block), lambda j: (0, 0, at(j))),
             whole((tokens, width)), whole((tokens, width)), whole((8, width)),
         ],
         out_shape=[
@@ -1286,15 +1420,23 @@
             jax.ShapeDtypeStruct((tokens, width), BF16),
             jax.ShapeDtypeStruct((8, width), F32),
         ],
-        scratch_shapes=[pltpu.VMEM((tokens, width), F32), pltpu.VMEM((tokens, width), F32)],
+        scratch_shapes=[
+            pltpu.VMEM((3, width, inner), BF16),
+            pltpu.VMEM((tokens, inner), BF16),
+            pltpu.VMEM((tokens, inner), BF16),
+            pltpu.VMEM((tokens, inner), BF16),
+            pltpu.VMEM((tokens, width), F32),
+            pltpu.VMEM((tokens, width), F32),
+            pltpu.SemaphoreType.DMA((3, blocks)),
+        ],
         compiler_params=params(),
         cost_estimate=cost(12 * tokens * width * inner, 3e7),
         name="feed_forward",
-    )(hidden, d_out, y1, gain, turn, weights, weights, weights)
+    )(hidden, d_out, y1, gains, turn, weights)
 
 
 BLOCK = HC
-LEAD, EVERY = 5, 3
+LEAD, EVERY = 7, 3
 
 
 def other_index(step):
@@ -1335,12 +1477,12 @@
     dout_any, hmid_any, hidden_any, x_any, dy_any, turn_any, dres_ref,
     act_ref, tail_ref, dgu_ref, gated_ref, wout_ref, attn_ref, gpre_ref, gain_ref, resp_ref, win_ref, wl_ref,
     gains_ref, dffn_ref,
-    p_ref, taps_ref, logit_ref, par_ref, cols_ref, back_ref, segr_ref, sin_ref, maps_ref,
+    p_ref, taps_q_ref, taps_k_ref, taps_v_ref, logit_ref, par_ref, cols_ref, back_ref, segr_ref, sin_ref, maps_ref,
     inv_ref, upd_ref, st_ref, stm_ref, amap_ref, rmap_ref,
     sum_ref, dx_ref, small_ref,
-    dlogit_ref, dtaps_ref, dpar_ref, dgain_ref, dattn_ref, dgpre_ref, lgrad_ref, acc_ref, left_ref,
+    taps_ref, dlogit_ref, dtaps_ref, dpar_ref, dgain_ref, dattn_ref, dgpre_ref, lgrad_ref, acc_ref, left_ref,
     total_ref, other_ref,
-    beta_ref, decay_ref, cum_ref, pf_ref, pre_ref, dmix_ref,
+    beta_ref, decay_ref, cum_ref, pf_ref, pre_ref, dmix_ref, dstate_ref, dbeta_ref, ddecay_ref,
     turn_ref, dps_ref, halo_ref, grads_ref, halves_ref,
     core_keep, core_send, core_recv, near_keep, near_send, near_recv,
     z_keep, pair_send, pair_recv, cross_send, cross_recv, far_send, far_recv, done_ref,
@@ -1693,32 +1835,41 @@
             halves_ref[head] = (earlier.astype(F32) + mm(through, later, TN)).astype(BF16)
             give_half(head).start()
 
-    @pl.when((since >= -1) & (since < EVERY * H - 1) & (lax.rem(jnp.maximum(since + 1, 0), EVERY) == 0))
-    def _():
-        head = (since + 1) // EVERY
-
-        @pl.when(upper)
-        def _():
-            grads_ref[1, head] = jnp.zeros((DK, DV), BF16)
-            give_half(head).wait_send()
-
-        @pl.when(jnp.logical_not(upper))
-        def _():
-            give_half(head).wait_recv()
-
-        d_state = grads_ref[1, head].astype(F32)
-        nearer = grads_ref[0, head].astype(F32) + mm(maps_ref[1, head], d_state, TN)
-        d_state = jnp.where(second, d_state, nearer)
-        backward_head(
-            head, d_state, p_ref, taps_ref, logit_ref, par_ref, cols_ref, back_ref, segr_ref,
-            dattn_ref.at[head], sin_ref, inv_ref, upd_ref, st_ref, stm_ref, amap_ref, rmap_ref,
-            dps_ref, dlogit_ref, dtaps_ref, dpar_ref, beta_ref, decay_ref, cum_ref, pf_ref, pre_ref, dmix_ref,
-        )
-        total_ref[0, pl.ds(pl.multiple_of(head * 8, 8), 8), :] = dtaps_ref[...]
-
-        @pl.when(place > 0)
-        def _():
-            give_halo(head).start()
+    ahead = since + EVERY
+    for phase in range(PHASES):
+
+        @pl.when((ahead >= 0) & (ahead < EVERY * H) & (lax.rem(jnp.maximum(ahead, 0), EVERY) == phase))
+        def _(phase=phase):
+            head = ahead // EVERY
+
+            def entering():
+                @pl.when(upper)
+                def _():
+                    grads_ref[1, head] = jnp.zeros((DK, DV), BF16)
+                    give_half(head).wait_send()
+
+                @pl.when(jnp.logical_not(upper))
+                def _():
+                    give_half(head).wait_recv()
+
+                d_state = grads_ref[1, head].astype(F32)
+                nearer = grads_ref[0, head].astype(F32) + mm(maps_ref[1, head], d_state, TN)
+                return jnp.where(second, d_state, nearer)
+
+            if phase == 0:
+                join_taps(taps_ref, taps_q_ref, taps_k_ref, taps_v_ref)
+            backward_head(
+                phase, head, entering, p_ref, taps_ref, logit_ref, par_ref, cols_ref, back_ref, segr_ref,
+                dattn_ref.at[head], sin_ref, inv_ref, upd_ref, st_ref, stm_ref, amap_ref, rmap_ref,
+                dps_ref, dlogit_ref, dtaps_ref, dpar_ref, beta_ref, decay_ref, cum_ref, pf_ref, pre_ref, dmix_ref,
+                dstate_ref, dbeta_ref, ddecay_ref,
+            )
+            if phase == PHASES - 1:
+                total_ref[0, pl.ds(pl.multiple_of(head * 8, 8), 8), :] = dtaps_ref[...]
+
+                @pl.when(place > 0)
+                def _():
+                    give_halo(head).start()
 
     @pl.when(step == count)
     def _():
@@ -1829,7 +1980,7 @@
     anywhere = pl.BlockSpec(memory_space=pl.ANY)
     whole = lambda shape: pl.BlockSpec(shape, lambda s: (0,) * len(shape))
     once = lambda shape: pl.BlockSpec(shape, lambda s: (0,) * len(shape), pipeline_mode=pl.Buffered(1))
-    coming = lambda s: jnp.clip((s + EVERY - LEAD) // EVERY, 0, H - 1)
+    coming = lambda s: jnp.clip((s - (LEAD - EVERY)) // EVERY, 0, H - 1)
     starting = lambda s: jnp.minimum(s, H - 1)
     by_head = lambda shape: pl.BlockSpec(shape, lambda s: (coming(s),) + (0,) * (len(shape) - 1))
     across = lambda shape, at: pl.BlockSpec(shape, lambda s: (0, at(s)))
@@ -1865,7 +2016,7 @@
             once((8, width)),
             once((8, width)),
             across((rows, HC), coming),
-            across((8, HC), coming),
+            *taps_specs(coming),
             once((rows, LANES)),
             once((8, LANES)),
             once((tokens, LANES)),
@@ -1887,6 +2038,7 @@
             jax.ShapeDtypeStruct((small, BLOCK), F32),
         ],
         scratch_shapes=[
+            pltpu.VMEM((8, HC), F32),
             pltpu.VMEM((tokens, LANES), F32),
             pltpu.VMEM((8, HC), F32),
             pltpu.VMEM((8, LANES), F32),
@@ -1904,6 +2056,9 @@
             pltpu.VMEM((rows, HC), F32),
             pltpu.VMEM((tokens, HC), F32),
             pltpu.VMEM((rows + 8, HC), F32),
+            pltpu.VMEM((chunks, DK, DV), F32),
+            pltpu.VMEM((tokens, LANES), F32),
+            pltpu.VMEM((tokens, LANES), F32),
             pltpu.VMEM((4, width, tokens), BF16),
             pltpu.VMEM((rows, HC), BF16),
             pltpu.VMEM((H, HALO, HC), BF16),
@@ -1934,13 +2089,27 @@
         name="reduce_gradients",
     )(
         d_out, hidden_mid, hidden, x, d_y, turn, d_mixer, act, act, d_gu, gated, weights, attn, gpre, gain_out, resp,
-        weights, weights, gains, d_ffn, proj, taps, logits, par, cols, back, segr, state_in, maps, *saved,
+        weights, weights, gains, d_ffn, proj, taps, taps, taps, logits, par, cols, back, segr, state_in, maps, *saved,
     )
 
 
 def unpack_kernel(
-    sum_ref, query_ref, key_ref, value_ref, gate_ref, logit_ref, out_ref, wg_ref, wu_ref, wd_ref, *, blocks
+    sum_ref, small_ref, dx_ref, query_ref, key_ref, value_ref, gate_ref, logit_ref, out_ref, wg_ref, wu_ref, wd_ref,
+    taps_ref, mix_ref, ffn_ref, norm_ref, par_ref, dx_out, *, blocks
 ):
+    dx_out[...] = dx_ref[...]
+    for h in range(H):
+        part = small_ref[8 * h : 8 * h + CONV, :]
+        taps_ref[:, h * DK : (h + 1) * DK] = part[:, :DK]
+        taps_ref[:, (H + h) * DK : (H + h + 1) * DK] = part[:, DK : 2 * DK]
+        taps_ref[:, 2 * H * DK + h * DV : 2 * H * DK + (h + 1) * DV] = part[:, 2 * DK :]
+    for row, ref in enumerate((mix_ref, ffn_ref)):
+        for n in range(2):
+            at = 8 * H + 8 * n + row
+            ref[:, n * small_ref.shape[1] : (n + 1) * small_ref.shape[1]] = small_ref[at : at + 1, :]
+    norm_ref[...] = small_ref[8 * H + 16 : 8 * H + 17, :DV]
+    par_ref[...] = small_ref[8 * H + 16 : 8 * H + 24, DV : DV + LANES]
+
     def part(n, low=0, high=BLOCK):
         return sum_ref[:, n * BLOCK + low : n * BLOCK + high].astype(F32)
 
@@ -1960,15 +2129,17 @@
         wd_ref[i * BLOCK : (i + 1) * BLOCK, :] = jnp.transpose(part(n))
     last, tail = blocks.count - 1, blocks.tail
     wd_ref[blocks.downs * BLOCK :, :] = jnp.transpose(part(last, 0, tail))
-    logit_ref[...] = part(last, tail, tail + LANES)
-
-
-def unpack_gradients(blocks, sums):
+    logit_ref[...] = jnp.transpose(part(last, tail, tail + LANES))[: 2 * H]
+
+
+def unpack_gradients(blocks, sums, small, d_inputs):
     rows = sums.shape[0]
     inner = blocks.downs * BLOCK + blocks.tail
+    width = d_inputs.shape[1]
     shapes = [
-        (rows, H * DK), (rows, H * DK), (rows, H * DV), (rows, H * DV), (rows, LANES), (H * DV, rows),
-        (rows, inner), (rows, inner), (inner, rows),
+        (rows, H * DK), (rows, H * DK), (rows, H * DV), (rows, H * DV), (2 * H, rows), (H * DV, rows),
+        (rows, inner), (rows, inner), (inner, rows), (CONV, H * HC), (1, width), (1, width), (1, DV), (8, LANES),
+        d_inputs.shape,
     ]
     return pl.pallas_call(
         functools.partial(unpack_kernel, blocks=blocks),
@@ -1976,7 +2147,7 @@
         compiler_params=params(),
         cost_estimate=cost(0, 6 * sums.size),
         name="unpack_gradients",
-    )(sums)
+    )(sums, small, d_inputs)
 
 
 def input_grad_kernel(
@@ -2098,19 +2269,23 @@
     low = lambda a: a.astype(BF16)
     inner = w_ffn_gate.shape[1]
     gain_out = out_norm_gain[None]
-    taps_parts = by_heads(conv_weight[:, : H * DK], conv_weight[:, H * DK : 2 * H * DK], conv_weight[:, 2 * H * DK :])
-    taps = jnp.pad(taps_parts, ((0, 8 - CONV), (0, 0)))
-    par = jnp.pad(jnp.stack([decay_log, dt_bias]), ((0, 6), (0, LANES - H)))
-    segr, later = token_rows(segments[0], place, tokens)
 
     if planned:
-        gains = jnp.pad(jnp.stack([norm_gain_mix, norm_gain_ffn]), ((0, 6), (0, 0)))
-        shards = (w_query, w_key, w_value, w_outgate, w_gates, w_out, w_ffn_gate, w_ffn_up, w_ffn_down)
-        outs = mixer_forward(inputs[0], cotangent[0], shards, gains, gain_out, taps, par, segr, later)
-        weights, hidden, x, d_out, turn, y1, hidden_mid, gains, cols, back, proj, logits, resp, *outs = outs
+        taps = conv_weight
+        shards = (w_query, w_key, w_value, w_outgate, w_gates.T, w_out, w_ffn_gate, w_ffn_up, w_ffn_down)
+        outs = mixer_forward(
+            inputs[0], cotangent[0], shards, (norm_gain_mix[None], norm_gain_ffn[None]), gain_out,
+            decay_log[None], dt_bias[None], segments, conv_weight,
+        )
+        weights, hidden, x, d_out, turn, y1, hidden_mid, gains, segr, par, cols, back, *outs = outs
+        proj, logits, resp, *outs = outs
         saved, (maps, state_in, attn, gpre, gated) = outs[:6], outs[6:]
-        gain_mix, gain_ffn = gains[0:1], gains[1:2]
+        gain_row = 1
     else:
+        taps = by_heads(conv_weight[:, : H * DK], conv_weight[:, H * DK : 2 * H * DK], conv_weight[:, 2 * H * DK :])
+        taps = jnp.pad(taps, ((0, 8 - CONV), (0, 0)))
+        par = jnp.pad(jnp.stack([decay_log, dt_bias]), ((0, 6), (0, LANES - H)))
+        segr, later = token_rows(segments[0], place, tokens)
         turn = jnp.eye(width, dtype=BF16)
         qkv = by_heads(low(w_query), low(w_key), low(w_value))
         qkv = jnp.concatenate([qkv[:, h * HC : (h + 1) * HC] for h in reversed(range(H))], axis=1)
@@ -2118,6 +2293,7 @@
         shard = [qkv, gates, low(w_outgate), low(w_out).T, low(w_ffn_gate), low(w_ffn_up), low(w_ffn_down).T]
         weights = lax.all_gather(jnp.concatenate(shard, axis=1), "dp", axis=0, tiled=True)
         gain_mix, gain_ffn = norm_gain_mix[None], norm_gain_ffn[None]
+        gains, gain_row = gain_ffn, 0
         cols = jnp.pad(segr.T, ((0, 0), (0, LANES - segr.shape[0])))
         back = jnp.pad(later.T[: tokens + HALO], ((0, 0), (0, LANES - later.shape[0])))
         x, d_out = inputs[0], cotangent[0]
@@ -2133,21 +2309,20 @@
             place_arr, slots, part, resp, exch, gpre, gain_out, weights, x, gain_ffn
         )
     result, act, d_gu, d_y, d_mixer, d_gain_ffn = feed_forward(
-        hidden_mid, d_out, y1, gain_ffn, turn, weights, inner
+        hidden_mid, d_out, y1, gains, gain_row, turn, weights, inner
     )
     if planned:
         blocks, (sums, d_inputs, small) = reduce_gradients(
             d_out, hidden_mid, hidden, x, d_y, turn, d_mixer, act, d_gu, gated, weights, attn, gpre, gain_out, resp,
             gains, d_gain_ffn, proj, taps, logits, par, cols, back, segr, state_in, maps, saved,
         )
-        g_query, g_key, g_value, g_og, g_gates, g_out, g_gate, g_up, g_down = unpack_gradients(blocks, sums)
-        d_taps = small[: 8 * H].reshape(H, 8, HC)[:, :CONV].transpose(1, 0, 2).reshape(CONV, H * HC)
-        rest = small[8 * H :]
-        d_gains = jnp.concatenate([rest[:2], rest[8:10]], axis=1)
-        d_gain_mix, d_gain_ffn = d_gains[0], d_gains[1]
-        d_gain_out, d_par = rest[16, :DV], rest[16:18, DV : DV + H]
-        d_conv = jnp.concatenate(from_heads(d_taps), axis=1)
-        d_decay_log, d_dt_bias = d_par[0], d_par[1]
+        (
+            g_query, g_key, g_value, g_og, g_gates, g_out, g_gate, g_up, g_down,
+            d_conv, d_gain_mix, d_gain_ffn, d_gain_out, d_par, d_inputs,
+        ) = unpack_gradients(blocks, sums, small, d_inputs)
+        g_gates = g_gates.T
+        d_gain_mix, d_gain_ffn, d_gain_out = d_gain_mix[0], d_gain_ffn[0], d_gain_out[0]
+        d_decay_log, d_dt_bias = d_par[0, :H], d_par[1, :H]
     else:
         d_attn, d_gpre, local_grad, d_gain_out = mixer_back(d_mixer, weights, attn, gpre, gain_out, resp)
         grads = lax.all_gather(local_grad, "seq")

time: 465 us -> 431 us (0.927)
  local copies, waits for them, and re-layouts: 14.6 us -> 1.27 us
  Pallas kernels: 438 us -> 425 us
  other arithmetic: 5.51 us -> 0 us
    pallas_call x1, Pallas kernels: 239 us -> 227 us  [reduce_gradients(): pl.pallas_call(functools.partial(reduce_kernel, blocks=blocks), grid=(blo...]
    unnamed x8 -> x0, local copies, waits for them, and re-layouts: 6.89 us -> none
where the time goes in v1:
time: 431 us; the launch traced here: 427 us
  Pallas kernels  425 us (99%)
    pallas_call x1, Pallas kernels, reduce_gradients(): pl.pallas_call(functools.partial(reduce_kernel, blocks=blocks), grid=(blo...  227 us
    pallas_call x1, Pallas kernels, mixer_forward(): pl.pallas_call(functools.partial(mixer_forward_kernel, spans=spans, inner...  160 us
    pallas_call x1, Pallas kernels, feed_forward(): pl.pallas_call(functools.partial(ffn_kernel, inner=inner, block=block, ga...  30.9 us

profile of v1, /device:TPU:8, one launch (start us, length us, event | category | flops | bytes accessed | tf_op | source)
XLA Modules:
  0.0 427.3 jit_solution(9656425269920095709)
XLA Ops:
  0.7 160.4 %mixer_forward.1 = (bf16[1024,17152]{1,0:T(8,128)(2,1)}, bf16[528,1024]{1,0:T(8,128)(2,1)}, bf16[512,1024]{1,0:T(8,128)(2,1)}, bf16[512,1024]{1,0:T(8,128)(2,1)}...) custom-call(bf16[512,1024]{1,0:T(8,128)(2,1)} %bitcast.19, ...), custom_call_target="tpu_custom_call" | custom-call | flops 99999997952 | bytes 100000000 | tf_op jit(solution)/shard_map/mixer_forward/pallas_call | solution.py:837
  161.1 30.9 %feed_forward.1 = (bf16[512,1024]{1,0:T(8,128)(2,1)}, bf16[512,2816]{1,0:T(8,128)(2,1)}, bf16[2,512,2816]{2,1,0:T(8,128)(2,1)}, f32[512,1024]{1,0:T(8,128)}, bf1...) custom-call(bf16[512,1024]{1,0:T(8,128)(2,1)} %get-tuple-element.67.h_ref.hmid_any, ...), custom_call_target="tpu_custom_call" | custom-call | flops 17716740096 | bytes 30000000 | tf_op jit(solution)/shard_map/feed_forward/pallas_call | solution.py:1398
  192.0 226.6 %reduce_gradients.1 = (bf16[128,16896]{1,0:T(8,128)(2,1)}, f32[512,1024]{1,0:T(8,128)}, f32[88,512]{1,0:T(8,128)}) custom-call(bf16[512,1024]{1,0:T(8,128)(2,1)} %get-tuple-element.68.dout_ref.dout_any, bf16[512,1024]{1,0:T(8,128)(2,1)} %get-tuple-element.67.h_ref.hmid_any, bf16[528,1024]{1,0:T(8,128)(2,1)} %get-tuple-element.74.hidden_any, ...), custom_call_target="tpu_custom_call" | custom-call | flops 99999997952 | bytes 100000000 | tf_op jit(solution)/shard_map/reduce_gradients/pallas_call | solution.py:1997
  418.6 7.2 %unpack_gradients.1 = (f32[128,1024]{1,0:T(8,128)}, f32[128,1024]{1,0:T(8,128)}, f32[128,2048]{1,0:T(8,128)}, f32[128,2048]{1,0:T(8,128)}, f32[16,128]{1,0:T(8,1...) custom-call(bf16[128,16896]{1,0:T(8,128)(2,1)} %get-tuple-element.99, ...), custom_call_target="tpu_custom_call" | custom-call | bytes 12976128 | tf_op jit(solution)/shard_map/unpack_gradients/pallas_call | solution.py:2144
  425.8 1.3 slice_bitcast_fusion

commit v2 on v1

--- a/solution.py
+++ b/solution.py
@@ -224,9 +224,13 @@
     return spans
 
 
+TICKS = (((), (6,)), ((7,), (8,)), ((9,), (10,)), ((11,), (12,)), ((13,), ()), ((14,), ()), ((15,), ()), ((16,), (17,)), (18,), (19,), (20,), (21,), (22,), (23,), (24,), (25,))
+
+
 class Gathering:
+    HALVED = (0, 3, 5, 8, 10, 13, 15)
     STAGES = (0, 1, 2, 3, 5, 7, 8)
-    FIRST = ((0, 1, 2, 3, 4, 5, 6), (0, 1, 2, 3, 4, 6, 7))
+    FIRST = ((0, 1, 2, 3, 4, 4, 5), (0, 1, 2, 3, 4, 5, 6), (0, 1, 2, 3, 5, 6, 7))
 
     def __init__(self, spans, shard_ref, full_ref, sems, pack):
         self.spans, self.shard, self.full, self.pack = spans, shard_ref, full_ref, pack
@@ -252,17 +256,31 @@
             for q in range(SPOTS)
         ]
 
-    def copy(self, group, kind):
+    def axis(self, group):
+        return 1 + self.HALVED.index(group) % 2 if group in self.HALVED else 0
+
+    def parts(self, group):
+        return (0, 3 - self.axis(group)) if self.axis(group) else (0,)
+
+    def copy(self, group, kind, part=0):
         at, size = self.spans[group]
         cols = pl.ds(at, size)
         piece, full = self.piece, self.full
         block = PLANES * piece
         rows = lambda quarter: pl.ds(quarter * block + piece, block - piece)
+        axis, sent = self.axis(group), kind
         if kind < 6:
             read, step, written = ((0, 1, 1), (0, -1, 3), (1, 1, 2), (3, -1, 2), (2, 1, 3), (2, -1, 1))[kind]
-            source = self.quarter(0, cols) if read == 0 else full.at[read * piece : (read + 1) * piece, cols]
-            target = full.at[written * piece : (written + 1) * piece, cols]
-            to, arrival = device(planes=step % PLANES), written - 1
+            quarter = self.parts(group)[part]
+            slot = lambda n: full.at[quarter * block + n * piece : quarter * block + (n + 1) * piece, cols]
+            source = self.quarter(quarter, cols) if read == 0 else slot(read)
+            target = slot(written)
+            to, arrival = device(planes=step % PLANES), written - 1 + 7 * part
+            sent += 10 * part
+        elif kind < 8 and axis:
+            source = full.at[rows(self.parts(group)[kind - 6]), cols]
+            target = full.at[rows((axis, 3)[kind - 6]), cols]
+            to, arrival = device(spot=axis), kind - 3
         elif kind < 8:
             source = full.at[rows(0), cols]
             target = full.at[rows(kind - 5), cols]
@@ -279,7 +297,7 @@
         return pltpu.make_async_remote_copy(
             src_ref=source,
             dst_ref=target,
-            send_sem=self.send_sem.at[group, kind],
+            send_sem=self.send_sem.at[group, sent],
             recv_sem=self.recv_sem.at[group, arrival],
             device_id=to,
             device_id_type=pl.DeviceIdType.MESH,
@@ -292,12 +310,15 @@
     def start(self, group, kind):
         @pl.when(self.sends(kind))
         def _():
-            self.copy(group, kind).start()
-
-    def arrive(self, group, kind, condition):
-        @pl.when(condition)
-        def _():
-            self.copy(group, kind).wait_recv()
+            for part in range(len(self.parts(group))):
+                self.copy(group, kind, part).start()
+
+    def arrive(self, group, kind, condition=None):
+        def wait():
+            for part in range(len(self.parts(group))):
+                self.copy(group, kind, part).wait_recv()
+
+        wait() if condition is None else pl.when(condition)(wait)
 
     def tick(self, at):
         z = self.z
@@ -319,7 +340,7 @@
                 self.arrive(group, 1, z < 3)
                 self.start(group, 3)
             elif stage == 2:
-                self.copy(group, 2).wait_recv()
+                self.arrive(group, 2)
                 self.start(group, 4)
                 self.start(group, 5)
             elif stage == 3:
@@ -328,11 +349,12 @@
                 self.copy(group, 5 + by).start()
                 self.copy(group, 8 - by).start()
             elif stage == 4:
-                self.copy(group, 5 + by).wait_recv()
-                self.copy(group, 8).start()
+                if not self.axis(group):
+                    self.copy(group, 5 + by).wait_recv()
+                    self.copy(group, 8).start()
             elif stage == 5:
                 self.copy(group, 8 - by).wait_recv()
-                self.copy(group, 8).wait_recv()
+                self.copy(group, 5 + by if self.axis(group) else 8).wait_recv()
                 for local in self.own(group):
                     local.wait()
                 self.copy(group, 9).start()
@@ -345,9 +367,10 @@
 
                 @pl.when(self.sends(kind))
                 def _(group=group, kind=kind):
-                    self.copy(group, kind).wait_send()
-
-            for kind in range(6, 10):
+                    for part in range(len(self.parts(group))):
+                        self.copy(group, kind, part).wait_send()
+
+            for kind in (6, 7, 9) if self.axis(group) else (6, 7, 8, 9):
                 self.copy(group, kind).wait_send()
 
 
@@ -715,7 +738,8 @@
 
             @pl.when(head == h)
             def _(h=h):
-                gathering.tick(lead + 2 * h - 1)
+                for at in TICKS[h][0]:
+                    gathering.tick(at)
 
         load_head(
             head, hidden_ref, full_ref, par_ref, p_ref, logit_ref, beta_ref, decay_ref, cum_ref, w_ref, wl_ref, load_sem
@@ -726,7 +750,8 @@
 
                 @pl.when(head == h)
                 def _(h=h):
-                    gathering.tick(lead + 2 * h)
+                    for at in TICKS[h][1]:
+                        gathering.tick(at)
 
         join_taps(taps_ref, taps_q_ref, taps_k_ref, taps_v_ref)
         state = forward_head(
@@ -745,11 +770,12 @@
     @pl.when(step >= H)
     def _():
         head = step - H
-        for n, at in enumerate(range(lead + 2 * H - 1, final_tick)):
-
-            @pl.when(head == min(n, H - 1))
-            def _(at=at):
-                gathering.tick(at)
+        for h in range(H):
+
+            @pl.when(head == h)
+            def _(h=h):
+                for at in TICKS[H + h]:
+                    gathering.tick(at)
 
         @pl.when(head < H - 1)
         def _():
@@ -917,8 +943,8 @@
             pltpu.VMEM((8, segments.shape[1] + 2 * LANES), F32),
             pltpu.VMEM((8, tokens + LANES), F32),
             sem((6,)),
+            sem((len(spans), 16)),
             sem((len(spans), 10)),
-            sem((len(spans), 7)),
             sem((len(spans), SPOTS)),
             sem((2, H)),
             sem((2, H)),
@@ -1538,22 +1564,20 @@
             device(planes=planes),
         )
 
-    def target(n, which):
-        spot = place if which == 0 else flip_spot(place, 2 - lax.rem(n, 2))
-        return sum_ref.at[
-            pl.ds(pl.multiple_of(spot * piece, piece), piece), pl.ds(pl.multiple_of(n * BLOCK, BLOCK), BLOCK)
-        ]
-
-    def spread(n, which):
+    def bits(n):
+        pair = lax.rem(n, 2)
+        along_x, along_y = lax.rem(place, 2), place // 2
+        return (1 - pair) * along_x + pair * along_y, (1 - pair) * along_y + pair * along_x
+
+    def spread(n):
         slot = lax.rem(n, 4)
         return remote(
-            done_ref.at[slot, which], target(n, which), done_ss.at[slot, which], done_rs.at[n, which],
-            flip_to(1 + lax.rem(n, 2)),
-        )
-
-    def keep(n, which):
+            done_ref.at[slot], sum_ref.at[n, bits(n)[0]], done_ss.at[slot], done_rs.at[n], flip_to(1 + lax.rem(n, 2))
+        )
+
+    def keep(n):
         slot = lax.rem(n, 4)
-        return pltpu.make_async_copy(done_ref.at[slot, which], target(n, which), own_sem.at[slot, which])
+        return pltpu.make_async_copy(done_ref.at[slot], sum_ref.at[n, bits(n)[0]], own_sem.at[slot])
 
     upper = place // 2 == 1
     second = lax.rem(place, 2) == 1
@@ -1649,17 +1673,17 @@
     @at_stage(10, 4)
     def _(n, free):
         if free:
-            for which in range(2):
-                spread(n - 4, which).wait_send()
-                keep(n - 4, which).wait()
+            spread(n - 4).wait_send()
+            keep(n - 4).wait()
             return
         slot = lax.rem(n, 4)
         to_far(n).wait_recv()
+        other = bits(n)[1]
         for which in range(2):
             total = far_send[slot, which].astype(F32) + far_recv[slot, 1 - which].astype(F32)
-            done_ref[slot, which] = total.astype(BF16)
-            keep(n, which).start()
-            spread(n, which).start()
+            done_ref[slot, other + which - 2 * other * which] = total.astype(BF16)
+        spread(n).start()
+        keep(n).start()
 
     @at_stage(8, 4)
     def _(n, free):
@@ -1953,13 +1977,11 @@
                 to_cross(n, 0).wait_send()
                 to_cross(n, 1).wait_send()
 
-            for which in range(2):
-                spread(n, which).wait_send()
-                keep(n, which).wait()
+            spread(n).wait_send()
+            keep(n).wait()
 
         def arrived(n, carry):
-            for which in range(2):
-                spread(n, which).wait_recv()
+            spread(n).wait_recv()
             return carry
 
         lax.fori_loop(0, count, arrived, 0)
@@ -2033,7 +2055,7 @@
         ],
         out_specs=[anywhere, anywhere, whole((small, BLOCK))],
         out_shape=[
-            jax.ShapeDtypeStruct((SPOTS * piece, blocks.count * BLOCK), BF16),
+            jax.ShapeDtypeStruct((blocks.count, 2, 2, piece, BLOCK), BF16),
             jax.ShapeDtypeStruct((tokens, width), F32),
             jax.ShapeDtypeStruct((small, BLOCK), F32),
         ],
@@ -2080,7 +2102,7 @@
             pltpu.VMEM((4, 2, piece, BLOCK), BF16),
             sem((3,)), sem((4,)), sem((4,)), sem((4,)), sem((4,)), sem((4,)),
             sem((4, 2)), sem((blocks.count,)), sem((4,)), sem((4,)),
-            sem((4, 2)), sem((blocks.count, 2)), sem((4, 2)),
+            sem((4,)), sem((blocks.count,)), sem((4,)),
             sem((H,)), sem((H,)), sem((2, H)), sem((2, H)),
             sem((4 + 2 * SPOTS,)), sem((6,)), sem((6,)),
         ],
@@ -2111,7 +2133,11 @@
     par_ref[...] = small_ref[8 * H + 16 : 8 * H + 24, DV : DV + LANES]
 
     def part(n, low=0, high=BLOCK):
-        return sum_ref[:, n * BLOCK + low : n * BLOCK + high].astype(F32)
+        rows = []
+        for spot in range(SPOTS):
+            first, other = (spot % 2, spot // 2) if n % 2 == 0 else (spot // 2, spot % 2)
+            rows.append(sum_ref[n, first, other, :, low:high])
+        return jnp.concatenate(rows, axis=0).astype(F32)
 
     for h, n in enumerate(blocks.head_at):
         query_ref[:, h * DK : (h + 1) * DK] = part(n, 0, DK)
@@ -2133,7 +2159,7 @@
 
 
 def unpack_gradients(blocks, sums, small, d_inputs):
-    rows = sums.shape[0]
+    rows = SPOTS * sums.shape[3]
     inner = blocks.downs * BLOCK + blocks.tail
     width = d_inputs.shape[1]
     shapes = [

time: 431 us -> 423 us (0.981)
  Pallas kernels: 425 us -> 417 us
    pallas_call x1, Pallas kernels: 160 us -> 152 us  [mixer_forward(): pl.pallas_call(functools.partial(mixer_forward_kernel, spans=spans, inner...]
where the time goes in v2:
time: 423 us; the launch traced here: 420 us
  Pallas kernels  417 us (99%)
    pallas_call x1, Pallas kernels, reduce_gradients(): pl.pallas_call(functools.partial(reduce_kernel, blocks=blocks), grid=(blo...  227 us
    pallas_call x1, Pallas kernels, mixer_forward(): pl.pallas_call(functools.partial(mixer_forward_kernel, spans=spans, inner...  152 us
    pallas_call x1, Pallas kernels, feed_forward(): pl.pallas_call(functools.partial(ffn_kernel, inner=inner, block=block, ga...  30.9 us

profile of v2, /device:TPU:8, one launch (start us, length us, event | category | flops | bytes accessed | tf_op | source)
XLA Modules:
  0.0 419.6 jit_solution(16848807395096552719)
XLA Ops:
  0.7 152.1 %mixer_forward.1 = (bf16[1024,17152]{1,0:T(8,128)(2,1)}, bf16[528,1024]{1,0:T(8,128)(2,1)}, bf16[512,1024]{1,0:T(8,128)(2,1)}, bf16[512,1024]{1,0:T(8,128)(2,1)}...) custom-call(bf16[512,1024]{1,0:T(8,128)(2,1)} %bitcast.19, ...), custom_call_target="tpu_custom_call" | custom-call | flops 99999997952 | bytes 100000000 | tf_op jit(solution)/shard_map/mixer_forward/pallas_call | solution.py:863
  152.7 30.9 %feed_forward.1 = (bf16[512,1024]{1,0:T(8,128)(2,1)}, bf16[512,2816]{1,0:T(8,128)(2,1)}, bf16[2,512,2816]{2,1,0:T(8,128)(2,1)}, f32[512,1024]{1,0:T(8,128)}, bf1...) custom-call(bf16[512,1024]{1,0:T(8,128)(2,1)} %get-tuple-element.67.h_ref.hmid_any, ...), custom_call_target="tpu_custom_call" | custom-call | flops 17716740096 | bytes 30000000 | tf_op jit(solution)/shard_map/feed_forward/pallas_call | solution.py:1424
  183.7 227.0 %reduce_gradients.1 = (bf16[33,2,2,32,512]{4,3,2,1,0:T(8,128)(2,1)}, f32[512,1024]{1,0:T(8,128)}, f32[88,512]{1,0:T(8,128)}) custom-call(bf16[512,1024]{1,0:T(8,128)(2,1)} %get-tuple-element.68.dout_ref.dout_any, bf16[512,1024]{1,0:T(8,128)(2,1)} %get-tuple-element.67.h_ref.hmid_any, bf16[528,1024]{1,0:T(8,128)(2,1)} %get-tuple-element.74.hidden_any, ...), custom_call_target="tpu_custom_call" | custom-call | flops 99999997952 | bytes 100000000 | tf_op jit(solution)/shard_map/reduce_gradients/pallas_call | solution.py:2019
  410.7 7.4 %unpack_gradients.1 = (f32[128,1024]{1,0:T(8,128)}, f32[128,1024]{1,0:T(8,128)}, f32[128,2048]{1,0:T(8,128)}, f32[128,2048]{1,0:T(8,128)}, f32[16,128]{1,0:T(8,1...) custom-call(bf16[33,2,2,32,512]{4,3,2,1,0:T(8,128)(2,1)} %get-tuple-, ...), custom_call_target="tpu_custom_call" | custom-call | bytes 12976128 | tf_op jit(solution)/shard_map/unpack_gradients/pallas_call | solution.py:2170
  418.1 1.3 slice_bitcast_fusion

commit v3 on v2

--- a/solution.py
+++ b/solution.py
@@ -1348,13 +1348,18 @@
 
 
 def ffn_kernel(
-    h_ref, dout_ref, y_ref, gain_ref, turn_ref, weights_ref,
+    h_ref, dout_ref, gain_ref, y_any, turn_any, weights_ref,
     out_ref, act_ref, dgu_ref, dy_ref, dmix_ref, dgain_ref,
-    w_ref, acts_ref, dg_ref, du_ref, res_ref, dh_ref, load_sem, *, inner, block, gain_row,
+    w_ref, acts_ref, dg_ref, du_ref, res_ref, dh_ref, y_ref, turn_ref, load_sem, late_sem,
+    *, inner, block, across, gain_row,
 ):
     step = pl.program_id(0)
     blocks = inner // block
-    across = dh_ref.shape[1] // (pl.num_programs(0) - blocks)
+    ends = blocks + dh_ref.shape[1] // across
+    late = [
+        pltpu.make_async_copy(source, to, late_sem.at[n])
+        for n, (source, to) in enumerate(((y_any, y_ref), (turn_any, turn_ref)))
+    ]
 
     def load(which, n):
         cols = pl.multiple_of(n * block, block)
@@ -1369,6 +1374,13 @@
         for n in range(blocks):
             for which in range(3):
                 load(which, n).start()
+        for copy in late:
+            copy.start()
+
+    @pl.when(step == blocks)
+    def _():
+        for copy in late:
+            copy.wait()
 
     @pl.when(step < blocks)
     def _():
@@ -1391,23 +1403,28 @@
         dgu_ref[1] = d_up
         du_ref[:, cols] = d_up
 
-    @pl.when(step >= blocks)
+    @pl.when((step >= blocks) & (step < ends))
     def _():
         rows = pl.ds(pl.multiple_of((step - blocks) * across, across), across)
         res_ref[:, rows] = y_ref[:, rows] + mm(acts_ref[...], w_ref[2, rows, :], NT)
         dh_ref[:, rows] = mm(dg_ref[...], w_ref[0, rows, :], NT) + mm(du_ref[...], w_ref[1, rows, :], NT)
 
-    @pl.when(step == pl.num_programs(0) - 1)
-    def _():
-        out_ref[...] = mm(res_ref[...], turn_ref[...], NT).astype(BF16)
-        value = y_ref[...]
+    @pl.when(step == ends)
+    def _():
+        dgain_ref[...] = jnp.zeros_like(dgain_ref)
+
+    @pl.when(step >= ends)
+    def _():
+        size = out_ref.shape[0]
+        rows = pl.ds(pl.multiple_of((step - ends) * size, size), size)
+        out_ref[...] = mm(res_ref[rows, :], turn_ref[...], NT).astype(BF16)
+        value = y_ref[rows, :]
         size = lax.rsqrt(jnp.mean(value * value, axis=-1, keepdims=True) + 1e-06)
         unit = value * size
-        d_hidden = dh_ref[...]
-        dgain_ref[...] = jnp.zeros_like(dgain_ref)
-        dgain_ref[0:1, :] = jnp.sum(d_hidden * unit, axis=0, keepdims=True)
+        d_hidden = dh_ref[rows, :]
+        dgain_ref[0:1, :] += jnp.sum(d_hidden * unit, axis=0, keepdims=True)
         d_unit = d_hidden * gain_ref[gain_row : gain_row + 1, :]
-        d_y = dout_ref[...].astype(F32) + size * (
+        d_y = dout_ref[rows, :].astype(F32) + size * (
             d_unit - unit * jnp.mean(d_unit * unit, axis=-1, keepdims=True)
         )
         dy_ref[...] = d_y
@@ -1416,27 +1433,27 @@
 
 def feed_forward(hidden, d_out, y1, gains, gain_row, turn, weights, inner):
     tokens, width = hidden.shape
-    block, across = 256, 256
+    block, across, part = 256, 512, 128
     blocks = inner // block
+    ends = blocks + width // across
     once = lambda shape: pl.BlockSpec(shape, lambda j: (0,) * len(shape), pipeline_mode=pl.Buffered(1))
     whole = lambda shape: pl.BlockSpec(shape, lambda j: (0,) * len(shape))
     at = lambda j: jnp.minimum(j, blocks - 1)
+    rows = pl.BlockSpec((part, width), lambda j: (jnp.maximum(j - ends, 0), 0))
     return pl.pallas_call(
-        functools.partial(ffn_kernel, inner=inner, block=block, gain_row=gain_row),
-        grid=(blocks + width // across,),
+        functools.partial(ffn_kernel, inner=inner, block=block, across=across, gain_row=gain_row),
+        grid=(ends + tokens // part,),
         in_specs=[
             once((tokens, width)),
             once((tokens, width)),
-            once((tokens, width)),
             once(gains.shape),
-            once((width, width)),
-            pl.BlockSpec(memory_space=pl.ANY),
-        ],
+        ]
+        + [pl.BlockSpec(memory_space=pl.ANY)] * 3,
         out_specs=[
-            whole((tokens, width)),
+            rows,
             pl.BlockSpec((tokens, block), lambda j: (0, at(j))),
             pl.BlockSpec((2, tokens, block), lambda j: (0, 0, at(j))),
-            whole((tokens, width)), whole((tokens, width)), whole((8, width)),
+            rows, rows, whole((8, width)),
         ],
         out_shape=[
             jax.ShapeDtypeStruct((tokens, width), BF16),
@@ -1453,16 +1470,19 @@
             pltpu.VMEM((tokens, inner), BF16),
             pltpu.VMEM((tokens, width), F32),
             pltpu.VMEM((tokens, width), F32),
+            pltpu.VMEM((tokens, width), F32),
+            pltpu.VMEM((width, width), BF16),
             pltpu.SemaphoreType.DMA((3, blocks)),
+            pltpu.SemaphoreType.DMA((2,)),
         ],
         compiler_params=params(),
         cost_estimate=cost(12 * tokens * width * inner, 3e7),
         name="feed_forward",
-    )(hidden, d_out, y1, gains, turn, weights)
+    )(hidden, d_out, gains, y1, turn, weights)
 
 
 BLOCK = HC
-LEAD, EVERY = 7, 3
+LEAD, EVERY = 8, 3
 
 
 def other_index(step):

time: 423 us -> 421 us (level)
  no operation moved by 1% of the time
where the time goes in v3:
time: 421 us; the launch traced here: 416 us
  Pallas kernels  414 us (98%)
    pallas_call x1, Pallas kernels, reduce_gradients(): pl.pallas_call(functools.partial(reduce_kernel, blocks=blocks), grid=(blo...  225 us
    pallas_call x1, Pallas kernels, mixer_forward(): pl.pallas_call(functools.partial(mixer_forward_kernel, spans=spans, inner...  152 us
    pallas_call x1, Pallas kernels, feed_forward(): pl.pallas_call(functools.partial(ffn_kernel, inner=inner, block=block, ac...  29.9 us

profile of v3, /device:TPU:8, one launch (start us, length us, event | category | flops | bytes accessed | tf_op | source)
XLA Modules:
  0.0 416.2 jit_solution(3783534043571239520)
XLA Ops:
  0.7 152.1 %mixer_forward.1 = (bf16[1024,17152]{1,0:T(8,128)(2,1)}, bf16[528,1024]{1,0:T(8,128)(2,1)}, bf16[512,1024]{1,0:T(8,128)(2,1)}, bf16[512,1024]{1,0:T(8,128)(2,1)}...) custom-call(bf16[512,1024]{1,0:T(8,128)(2,1)} %bitcast.19, ...), custom_call_target="tpu_custom_call" | custom-call | flops 99999997952 | bytes 100000000 | tf_op jit(solution)/shard_map/mixer_forward/pallas_call | solution.py:863
  152.7 29.9 %feed_forward.1 = (bf16[512,1024]{1,0:T(8,128)(2,1)}, bf16[512,2816]{1,0:T(8,128)(2,1)}, bf16[2,512,2816]{2,1,0:T(8,128)(2,1)}, f32[512,1024]{1,0:T(8,128)}, bf1...) custom-call(bf16[512,1024]{1,0:T(8,128)(2,1)} %get-tuple-element.67.h_ref.hmid_any, ...), custom_call_target="tpu_custom_call" | custom-call | flops 17716740096 | bytes 30000000 | tf_op jit(solution)/shard_map/feed_forward/pallas_call | solution.py:1443
  182.7 224.6 %reduce_gradients.1 = (bf16[33,2,2,32,512]{4,3,2,1,0:T(8,128)(2,1)}, f32[512,1024]{1,0:T(8,128)}, f32[88,512]{1,0:T(8,128)}) custom-call(bf16[512,1024]{1,0:T(8,128)(2,1)} %get-tuple-element.68.dout_ref.dout_any, bf16[512,1024]{1,0:T(8,128)(2,1)} %get-tuple-element.67.h_ref.hmid_any, bf16[528,1024]{1,0:T(8,128)(2,1)} %get-tuple-element.74.hidden_any, ...), custom_call_target="tpu_custom_call" | custom-call | flops 99999997952 | bytes 100000000 | tf_op jit(solution)/shard_map/reduce_gradients/pallas_call | solution.py:2039
  407.3 7.4 %unpack_gradients.1 = (f32[128,1024]{1,0:T(8,128)}, f32[128,1024]{1,0:T(8,128)}, f32[128,2048]{1,0:T(8,128)}, f32[128,2048]{1,0:T(8,128)}, f32[16,128]{1,0:T(8,1...) custom-call(bf16[33,2,2,32,512]{4,3,2,1,0:T(8,128)(2,1)} %get-tuple-, ...), custom_call_target="tpu_custom_call" | custom-call | bytes 12976128 | tf_op jit(solution)/shard_map/unpack_gradients/pallas_call | solution.py:2190
  414.7 1.3 slice_bitcast_fusion
